TPU v7x, 256 devices: a whole 4x4x8 slice. The times are simulated.
256 devices in a mesh: dp: 4 (over x_hi, core), ctx: 64 (over x_lo, y, z).
Axes of the slice: x: 4 (x_hi: 2, x_lo: 2; x = x_hi * 2 + x_lo), y: 4, z: 8, core: 2. Of those that a mesh axis runs over, the one named last changes fastest.
Arguments:
- tokens: int32 [4, 131072], P('dp', 'ctx'), may hold values from 0 to 255
- targets: int32 [4, 131072], P('dp', 'ctx'), may hold values from 0 to 255
- embed: bfloat16 [256, 256], replicated, may hold values from -6 to 6
- first_norm_gain: float32 [256], replicated, may hold values from 0.5 to 1.5
- first_kernel_weights: bfloat16 [3, 256, 512], replicated, may hold values from -0.21875 to 0.21875
- first_output_projection: bfloat16 [512, 256], replicated, may hold values from -0.25 to 0.25
- second_norm_gain: float32 [256], replicated, may hold values from 0.5 to 1.5
- second_kernel_weights: bfloat16 [3, 256, 512], replicated, may hold values from -0.21875 to 0.21875
- second_output_projection: bfloat16 [512, 256], replicated, may hold values from -0.25 to 0.25
- gain_final: float32 [256], replicated, may hold values from 0.5 to 1.5
- head: bfloat16 [256, 256], replicated, may hold values from -16 to 16
Outputs:
- token_loss: float32 [4, 131072], P('dp', 'ctx')
- grad_embed: float32 [256, 256], replicated
- first_norm_gain_gradient: float32 [256], replicated
- first_kernel_gradient: float32 [3, 256, 512], replicated
- first_projection_gradient: float32 [512, 256], replicated
- second_norm_gain_gradient: float32 [256], replicated
- second_kernel_gradient: float32 [3, 256, 512], replicated
- second_projection_gradient: float32 [512, 256], replicated
- grad_gain_final: float32 [256], replicated
- grad_head: float32 [256, 256], replicated
All inputs are finite; a program needn't handle non-finite values.
Results may differ from a plain program's by a relative error of at most 0.0037.
Values may be sent and summed in bfloat16 or wider, within the bound.
No kernel may reach another device: no remote copies, remote signals or barrier semaphores. Data moves between devices by JAX's collectives and lax.ppermute only.
A program may use at most 64 MiB of HBM per device.

v0:
```python
import functools

import jax
import jax.numpy as jnp
from jax import lax
from jax.experimental import pallas as pl
from jax.experimental.pallas import tpu as pltpu
from jax.sharding import Mesh, PartitionSpec as P

EPS = 1e-05
BF = jnp.bfloat16
F32 = jnp.float32
WIDE = 256
HALF = 2560
LEAD = 128
CHUNK = 1024


def rows_dot(left, right):
    return lax.dot_general(left, right, (((0,), (0,)), ((), ())), preferred_element_type=F32)

def cols_dot(left, right):
    return lax.dot_general(left, right, (((1,), (1,)), ((), ())), preferred_element_type=F32)

def dot(left, right):
    return jnp.dot(left, right, preferred_element_type=F32)

def mean(v):
    return jnp.sum(v, axis=-1, keepdims=True) * (1.0 / WIDE)

def kernel(step, chunk, loss_scale, core_ref, toks_ref, targs_ref, embed_ref, gain1_ref, taps1_ref, out1_ref, gain2_ref, taps2_ref,
           out2_ref, gainf_ref, head_ref, loss_ref, keep_ref,
           x0_ref, h1_ref, a1_ref, x1_ref, h2_ref, a2_ref, gx2_ref, gc2_ref, gc1_ref, lossT_ref):
    rows = x0_ref.shape[0]
    n = rows // chunk
    blocks = chunk // 128
    core = core_ref[0]
    one = core
    two = 1 - core
    zeros = jnp.zeros((LEAD, WIDE), BF)
    h1_ref[0:LEAD, :] = zeros
    h2_ref[0:LEAD, :] = zeros
    gc1_ref[rows:rows + LEAD, :] = jnp.zeros((LEAD, 2 * WIDE), BF)
    gc2_ref[rows:rows + LEAD, :] = jnp.zeros((LEAD, 2 * WIDE), BF)
    keep_ref[...] = jnp.zeros_like(keep_ref)
    tokT = toks_ref[...].T
    targT = targs_ref[...].T
    letters = lax.broadcasted_iota(jnp.int32, (128, WIDE), 1)
    column = lax.broadcasted_iota(jnp.int32, tokT.shape, 1)

    def choose(table, i):
        cols = [jnp.sum(jnp.where(column == i * blocks + b, table, 0), axis=1, keepdims=True) for b in range(blocks)]
        return cols

    def forward(i, carry):
        t0 = pl.multiple_of(i * chunk, chunk)
        here = pl.ds(t0, chunk)
        onehot = jnp.concatenate([(c == letters).astype(F32).astype(BF) for c in choose(tokT, i)], axis=0)
        x0 = dot(onehot, embed_ref[...])
        x0_ref[here, :] = x0.astype(BF)
        s = lax.rsqrt(mean(x0 * x0) + EPS)
        h = jnp.maximum(x0 * s * gain1_ref[...], 0.0).astype(BF)
        h1_ref[pl.ds(t0 + LEAD, chunk), :] = h
        hs = jnp.concatenate([h, h1_ref[pl.ds(t0 + LEAD - step, chunk), :], h1_ref[pl.ds(t0 + LEAD - 2 * step, chunk), :]], axis=1)
        a = jnp.maximum(dot(hs, taps1_ref[...]), 0.0).astype(BF)
        a1_ref[here, :] = a
        x1 = x0 + dot(a, out1_ref[...])
        x1_ref[here, :] = x1
        s = lax.rsqrt(mean(x1 * x1) + EPS)
        h = jnp.maximum(x1 * s * gain2_ref[...], 0.0).astype(BF)
        h2_ref[pl.ds(t0 + LEAD, chunk), :] = h
        hs = jnp.concatenate([h, h2_ref[pl.ds(t0 + LEAD - 2 * step, chunk), :], h2_ref[pl.ds(t0 + LEAD - 4 * step, chunk), :]], axis=1)
        a = jnp.maximum(dot(hs, taps2_ref[...]), 0.0).astype(BF)
        a2_ref[here, :] = a
        x2 = x1 + dot(a, out2_ref[...])
        s = lax.rsqrt(mean(x2 * x2) + EPS)
        normed = x2 * s
        final = (normed * gainf_ref[...]).astype(BF)
        logits = dot(final, head_ref[...])
        highest = jnp.max(logits, axis=1, keepdims=True)
        e = jnp.exp(logits - highest)
        total = jnp.sum(e, axis=1, keepdims=True)
        wanted = jnp.concatenate([(c == letters).astype(F32) for c in choose(targT, i)], axis=0)
        loss = highest + jnp.log(total) - jnp.sum(logits * wanted, axis=1, keepdims=True)
        place = lax.broadcasted_iota(jnp.int32, lossT_ref.shape, 1)
        for b in range(blocks):
            lossT_ref[...] = jnp.where(place == i * blocks + b, loss[b * 128:(b + 1) * 128], lossT_ref[...])
        gl = ((e * (1.0 / total) - wanted) * loss_scale).astype(BF)
        keep_ref[two, 0:256, :] += rows_dot(final, gl)
        gfin = cols_dot(gl, head_ref[...])
        keep_ref[two, 2305:2306, :] += jnp.sum(gfin * normed, axis=0, keepdims=True)
        w = gfin * gainf_ref[...]
        gx2 = s * (w - normed * mean(w * normed))
        gx2_ref[here, :] = gx2
        low = gx2.astype(BF)
        keep_ref[two, 1792:2304, :] += rows_dot(a, low)
        gact = cols_dot(low, out2_ref[...])
        gc2_ref[here, :] = jnp.where(a > 0, gact, 0.0).astype(BF)
        return carry

    lax.fori_loop(0, n, forward, 0)
    loss_ref[...] = lossT_ref[...].T

    def back(i, carry):
        j = n - 1 - i
        t0 = pl.multiple_of(j * chunk, chunk)
        here = pl.ds(t0, chunk)

        def block(g, x, h, gc_ref, slot, taps_ref, gain, dist):
            gcs = [gc_ref[pl.ds(t0 + k * dist, chunk), :] for k in range(3)]
            gh = sum(cols_dot(gcs[k], taps_ref[k * WIDE:(k + 1) * WIDE, :]) for k in range(3))
            for k in range(3):
                part = rows_dot(h, gcs[k])
                keep_ref[slot, 256 + 512 * k:512 + 512 * k, :] += part[:, :WIDE]
                keep_ref[slot, 512 + 512 * k:768 + 512 * k, :] += part[:, WIDE:]
            gn = jnp.where(h > 0, gh, 0.0)
            s = lax.rsqrt(mean(x * x) + EPS)
            normed = x * s
            keep_ref[slot, 2304:2305, :] += jnp.sum(gn * normed, axis=0, keepdims=True)
            w = gn * gain
            return g + s * (w - normed * mean(w * normed))

        gx1 = block(gx2_ref[here, :], x1_ref[here, :], h2_ref[pl.ds(t0 + LEAD, chunk), :], gc2_ref, two, taps2_ref, gain2_ref[...], 2 * step)
        low = gx1.astype(BF)
        a = a1_ref[here, :]
        keep_ref[one, 1792:2304, :] += rows_dot(a, low)
        gact = cols_dot(low, out1_ref[...])
        gc1_ref[here, :] = jnp.where(a > 0, gact, 0.0).astype(BF)
        gx0 = block(gx1, x0_ref[here, :].astype(F32), h1_ref[pl.ds(t0 + LEAD, chunk), :], gc1_ref, one, taps1_ref, gain1_ref[...], step)
        up = lax.broadcasted_iota(jnp.int32, (WIDE, 128), 0)
        toks_here = toks_ref[pl.ds(j * blocks, blocks), :]
        onehotT = jnp.concatenate([(up == toks_here[b:b + 1, :]).astype(F32).astype(BF) for b in range(blocks)], axis=1)
        keep_ref[one, 0:256, :] += dot(onehotT, gx0.astype(BF))
        return carry

    lax.fori_loop(0, n, back, 0)


def compute(core, toks, targs, embed, g1, taps1, out1, g2, taps2, out2, gf, head, loss_scale, step, chunk=CHUNK):
    rows = toks.size
    vm = lambda *s: pltpu.VMEM(s[:-1], s[-1])
    return pl.pallas_call(
        functools.partial(kernel, step, chunk, loss_scale),
        out_shape=(jax.ShapeDtypeStruct((rows // 128, 128), F32), jax.ShapeDtypeStruct((2, HALF, WIDE), F32)),
        in_specs=[pl.BlockSpec(memory_space=pltpu.SMEM)] + [pl.BlockSpec(memory_space=pltpu.VMEM)] * 11,
        out_specs=(pl.BlockSpec(memory_space=pltpu.VMEM), pl.BlockSpec(memory_space=pltpu.VMEM)),
        scratch_shapes=[
            vm(rows, WIDE, BF), vm(rows + LEAD, WIDE, BF), vm(rows, 2 * WIDE, BF), vm(rows, WIDE, F32),
            vm(rows + LEAD, WIDE, BF), vm(rows, 2 * WIDE, BF), vm(rows, WIDE, F32), vm(rows + LEAD, 2 * WIDE, BF),
            vm(rows + LEAD, 2 * WIDE, BF), vm(128, rows // 128, F32),
        ],
        compiler_params=pltpu.CompilerParams(vmem_limit_bytes=50 * 2**20),
    )(core, toks.reshape(-1, 128), targs.reshape(-1, 128), embed, g1[None], taps1.reshape(-1, 512), out1, g2[None], taps2.reshape(-1, 512), out2, gf[None], head)


def pick(array, index):
    return lax.dynamic_index_in_dim(array, index, 0, keepdims=False)


def swap(array, axis, mask):
    count = lax.axis_size(axis)
    return lax.ppermute(array, axis, [(i, i ^ mask) for i in range(count)])


def scatter_sum(array, axis, dtype):
    count = lax.axis_size(axis)
    mine = lax.axis_index(axis)
    parts = array.reshape(count, -1, WIDE)
    total = pick(parts, mine)
    for k in range(1, count):
        sent = pick(parts, lax.rem(mine + k, count)).astype(dtype)
        got = lax.ppermute(sent, axis, [(i, (i + k) % count) for i in range(count)])
        total = total + got.astype(jnp.float32)
    return total


def gather(array, axis):
    count = lax.axis_size(axis)
    mine = lax.axis_index(axis)
    whole = jnp.zeros((count,) + array.shape, array.dtype)
    whole = lax.dynamic_update_index_in_dim(whole, array, mine, 0)
    for k in range(1, count):
        got = lax.ppermute(array, axis, [(i, (i + k) % count) for i in range(count)])
        whole = lax.dynamic_update_index_in_dim(whole, got, lax.rem(mine + count - k, count), 0)
    return whole.reshape(-1, WIDE)


X = ("x_hi", "x_lo")


def reduce_all(keep, send):
    total = keep + swap(send, "core", 1)
    total = scatter_sum(total, X, BF)
    total = scatter_sum(total, "y", BF)
    bit = lax.rem(lax.axis_index("z"), 2)
    pair = total.reshape(2, -1, WIDE)
    total = pick(pair, bit) + swap(pick(pair, 1 - bit), "z", 1)
    total = total + swap(total, "z", 2)
    total = total + swap(total, "z", 4)
    total = total.astype(BF)
    other = swap(total, "z", 1)
    total = jnp.where(bit == 0, jnp.concatenate([total, other]), jnp.concatenate([other, total]))
    total = gather(total, "y")
    total = gather(total, X)
    return total, swap(total, "core", 1)


def spread_kernel(core_ref, mine_ref, other_ref, *outs):
    even = core_ref[0] == 0

    def write(first, square, taps, out_w, gains):
        def rows(start, count):
            left, right = mine_ref[pl.ds(start, count), :], other_ref[pl.ds(start, count), :]
            return (jnp.where(even, left, right) if first else jnp.where(even, right, left)).astype(F32)

        square[...] = rows(0, 256)
        for k in range(3):
            taps[k, :, :WIDE] = rows(256 + 512 * k, 256)
            taps[k, :, WIDE:] = rows(512 + 512 * k, 256)
        out_w[...] = rows(1792, 512)
        tail = rows(2304, 16)
        for i, gain in enumerate(gains):
            gain[...] = tail[i : i + 1]

    embed, gain1, taps1, out1, gain2, taps2, out2, gainf, head = outs
    write(True, embed, taps1, out1, [gain1])
    write(False, head, taps2, out2, [gain2, gainf])


def spread(core, mine, other):
    vmem = pl.BlockSpec(memory_space=pltpu.VMEM)
    shapes = [(256, 256), (1, 256), (3, 256, 512), (512, 256), (1, 256), (3, 256, 512), (512, 256), (1, 256), (256, 256)]
    return pl.pallas_call(
        spread_kernel,
        out_shape=tuple(jax.ShapeDtypeStruct(s, F32) for s in shapes),
        in_specs=[pl.BlockSpec(memory_space=pltpu.SMEM), vmem, vmem],
        out_specs=(vmem,) * len(shapes),
        compiler_params=pltpu.CompilerParams(vmem_limit_bytes=32 * 2**20),
    )(core, mine, other)


def local(
    tokens,
    targets,
    embed,
    first_norm_gain,
    first_kernel_weights,
    first_output_projection,
    second_norm_gain,
    second_kernel_weights,
    second_output_projection,
    gain_final,
    head,
):
    ctx = ("x_lo", "y", "z")
    shards = lax.axis_size(ctx)
    count = tokens.shape[1]
    step = count // shards
    loss_scale = float(count * shards * lax.axis_size(("x_hi", "core"))) ** (-0.5)
    both = jnp.concatenate([tokens.reshape(shards, step), targets.reshape(shards, step)], axis=1)
    both = lax.all_to_all(both, ctx, 0, 0, tiled=True)
    core = lax.axis_index("core").reshape(1)
    loss, packed = compute(
        core,
        both[:, :step],
        both[:, step:],
        embed,
        first_norm_gain,
        first_kernel_weights,
        first_output_projection,
        second_norm_gain,
        second_kernel_weights,
        second_output_projection,
        gain_final,
        head,
        loss_scale,
        step,
    )
    loss = lax.all_to_all(loss.reshape(shards, step), ctx, 0, 0, tiled=True)
    mine, other = reduce_all(packed[0], packed[1])
    grad_embed, gain1, taps1, out1, gain2, taps2, out2, gainf, grad_head = spread(core, mine, other)
    return (
        loss.reshape(1, count),
        grad_embed,
        gain1[0],
        taps1,
        out1,
        gain2[0],
        taps2,
        out2,
        gainf[0],
        grad_head,
    )


def solution(mesh):
    fine = Mesh(mesh.devices.reshape(2, 2, 2, 4, 8), ("x_hi", "core", "x_lo", "y", "z"))
    data = P(("x_hi", "core"), ("x_lo", "y", "z"))
    in_specs = (data, data, P(), P(), P(), P(), P(), P(), P(), P(), P())
    out_specs = (data, P(), P(), P(), P(), P(), P(), P(), P(), P())
    return jax.shard_map(local, mesh=fine, in_specs=in_specs, out_specs=out_specs, check_vma=False)
```

profile of v0, /device:TPU:33, one launch (start us, length us, event | category | flops | bytes accessed | tf_op | source)
XLA Modules:
  0.0 163.2 jit_solution(165633167096560728)
XLA Ops:
  0.6 0.5 broadcast.29
  1.2 1.4 reduce.10
  2.5 0.1 reshape.129
  2.6 1.4 reduce.9
  4.0 0.1 reshape.130
  4.0 0.7 pad_add_fusion
  4.7 12.1 %all-to-all-start = ((s32[64,1,64]{2,1,0:T(1,128)}), s32[64,1,64]{2,1,0:T(1,128)S(1)}, u32[]{:S(2)}, u32[]{:S(2)}) async-start(s32[64,1,64]{2,1,0:T(1,128)} %bitcast.2), calls=%async_computation | async-start | bytes 65536 | tf_op jit(solution)/shard_map/all_to_all | solution.py:261
  16.9 8.6 %all-to-all-done = s32[64,1,64]{2,1,0:T(1,128)S(1)} async-done(((s32[64,1,64]{2,1,0:T(1,128)}), s32[64,1,64]{2,1,0:T(1,128)S(1)}, u32[]{:S(2)}, u32[]{:S(2)}) %all-to-all-start) | async-done | bytes 16416 | tf_op jit(solution)/shard_map/all_to_all | solution.py:261
  25.5 0.1 fusion.11
  25.5 0.1 reshape.131.toks_ref
  25.6 0.1 reshape.132.targs_ref
  25.7 1.1 copy-done
  26.8 1.1 copy-done.1
  28.0 0.9 copy-done.2
  28.9 0.9 copy-done.3
  29.9 0.9 copy-done.4
  30.8 0.9 copy-done.5
  31.7 0.7 copy-done.6
  32.3 0.7 copy-done.7
  33.0 0.7 copy-done.8
  33.7 22.8 %shard_map.186 = (f32[16,128]{1,0:T(8,128)S(1)}, f32[2,2560,256]{2,1,0:T(8,128)}) custom-call(s32[1]{0:T(128)} %bitcast.core_ref, s32[16,128]{1,0:T(8,128)S(1)} %reshape.131.toks_ref, s32[16,128]{1,0:T(8,128)S(1)} %reshape.132.targs_ref, bf16[256,256]{1,0:T(8,128)(2,1)S(1)} %copy-done.4, f32[1,256]{1,0:T(1,128)S(1)} %bitcast.72, ...), custom_call_target="tpu_custom_call" | custom-call | tf_op jit(solution)/shard_map/pallas_call | solution.py:142
  56.5 1.9 %slice_bitcast_fusion = f32[2560,256]{1,0:T(8,128)S(1)} fusion(f32[2,2560,256]{2,1,0:T(8,128)} %get-tuple-element.22), kind=kLoop, calls=%fused_computation.1 | loop fusion | bytes 5242880 | tf_op jit(solution)/shard_map/squeeze | solution.py:280
  58.4 2.2 %collective-permute-start = (f32[2560,256]{1,0:T(8,128)S(1)}, f32[2560,256]{1,0:T(8,128)}, u32[]{:S(2)}, u32[]{:S(2)}) collective-permute-start(f32[2560,256]{1,0:T(8,128)S(1)} %slice_bitcast_fusion), channel_id=1, source_target_pairs={{0,64},{64,0},{1,65},{65,1},{2,66},{66,2},{3,67},{67,3},{4,68},{68... | collective-permute-start | bytes 7864328 | tf_op jit(solution)/shard_map/ppermute | solution.py:162
  60.6 4.7 %collective-permute-done = f32[2560,256]{1,0:T(8,128)} collective-permute-done((f32[2560,256]{1,0:T(8,128)S(1)}, f32[2560,256]{1,0:T(8,128)}, u32[]{:S(2)}, u32[]{:S(2)}) %collective-permute-start) | collective-permute-done | bytes 2621472 | tf_op jit(solution)/shard_map/ppermute | solution.py:162
  65.3 2.9 %bitcast_add_fusion = f32[2560,256]{1,0:T(8,128)S(1)} fusion(f32[2560,256]{1,0:T(8,128)} %collective-permute-done, f32[2,2560,256]{2,1,0:T(8,128)} %get-tuple-element.22), kind=kLoop, calls=%fused_computation | loop fusion | flops 655360 | bytes 7864320 | tf_op jit(solution)/shard_map/add | solution.py:192
  68.2 1.0 fusion.2
  69.2 0.5 collective-permute-start.1
  69.6 2.5 %collective-permute-start.2 = (bf16[640,256]{1,0:T(8,128)(2,1)}, bf16[640,256]{1,0:T(8,128)(2,1)S(1)}, u32[]{:S(2)}, u32[]{:S(2)}) collective-permute-start(bf16[640,256]{1,0:T(8,128)(2,1)} %get-tuple-element.34), channel_id=1, source_target_pairs={{0,128},{32,160},{128,0},{160,32},{1,129},{33,161},{129,1},{161,33... | collective-permute-start | bytes 983048 | tf_op jit(solution)/shard_map/ppermute | solution.py:172
  72.1 1.6 collective-permute-start.3
  73.7 5.8 %collective-permute-done.1 = bf16[640,256]{1,0:T(8,128)(2,1)S(1)} collective-permute-done((bf16[640,256]{1,0:T(8,128)(2,1)}, bf16[640,256]{1,0:T(8,128)(2,1)S(1)}, u32[]{:S(2)}, u32[]{:S(2)}) %collective-permute-start.1) | collective-permute-done | bytes 327712 | tf_op jit(solution)/shard_map/ppermute | solution.py:172
  79.5 7.3 %collective-permute-done.2 = bf16[640,256]{1,0:T(8,128)(2,1)S(1)} collective-permute-done((bf16[640,256]{1,0:T(8,128)(2,1)}, bf16[640,256]{1,0:T(8,128)(2,1)S(1)}, u32[]{:S(2)}, u32[]{:S(2)}) %collective-permute-start.2) | collective-permute-done | bytes 327712 | tf_op jit(solution)/shard_map/ppermute | solution.py:172
  86.8 0.7 copy-done.10
  87.5 1.4 fusion.1
  88.9 0.4 collective-permute-start.4
  89.3 1.5 collective-permute-start.5
  90.9 1.0 collective-permute-start.6
  91.9 2.8 %collective-permute-done.4 = bf16[160,256]{1,0:T(8,128)(2,1)S(1)} collective-permute-done((bf16[160,256]{1,0:T(8,128)(2,1)S(1)}, bf16[160,256]{1,0:T(8,128)(2,1)S(1)}, u32[]{:S(2)}, u32[]{:S(2)}) %collective-permute-start.4) | collective-permute-done | bytes 81952 | tf_op jit(solution)/shard_map/ppermute | solution.py:172
  94.7 0.5 collective-permute-done.6
  95.3 1.2 collective-permute-start.7
  96.6 2.1 %collective-permute-done.7 = f32[80,256]{1,0:T(8,128)S(1)} collective-permute-done((f32[80,256]{1,0:T(8,128)S(1)}, f32[80,256]{1,0:T(8,128)S(1)}, u32[]{:S(2)}, u32[]{:S(2)}) %collective-permute-start.7) | collective-permute-done | bytes 81952 | tf_op jit(solution)/shard_map/ppermute | solution.py:162
  98.7 0.3 collective-permute-start.8
  99.1 4.0 %collective-permute-done.8 = f32[80,256]{1,0:T(8,128)S(1)} collective-permute-done((f32[80,256]{1,0:T(8,128)S(1)}, f32[80,256]{1,0:T(8,128)S(1)}, u32[]{:S(2)}, u32[]{:S(2)}) %collective-permute-start.8) | collective-permute-done | bytes 81952 | tf_op jit(solution)/shard_map/ppermute | solution.py:162
  103.1 1.5 collective-permute-start.9
  104.6 6.5 %collective-permute-done.9 = f32[80,256]{1,0:T(8,128)S(1)} collective-permute-done((f32[80,256]{1,0:T(8,128)S(1)}, f32[80,256]{1,0:T(8,128)S(1)}, u32[]{:S(2)}, u32[]{:S(2)}) %collective-permute-start.9) | collective-permute-done | bytes 81952 | tf_op jit(solution)/shard_map/ppermute | solution.py:162
  111.2 1.3 collective-permute-start.10
  112.4 1.9 %collective-permute-done.10 = bf16[80,256]{1,0:T(8,128)(2,1)S(1)} collective-permute-done((bf16[80,256]{1,0:T(8,128)(2,1)S(1)}, bf16[80,256]{1,0:T(8,128)(2,1)S(1)}, u32[]{:S(2)}, u32[]{:S(2)}) %collective-permute-start.10) | collective-permute-done | bytes 40992 | tf_op jit(solution)/shard_map/ppermute | solution.py:162
  114.3 1.4 collective-permute-start.11
  115.7 2.0 %collective-permute-start.12 = (bf16[160,256]{1,0:T(8,128)(2,1)S(1)}, bf16[160,256]{1,0:T(8,128)(2,1)S(1)}, u32[]{:S(2)}, u32[]{:S(2)}) collective-permute-start(bf16[160,256]{1,0:T(8,128)(2,1)S(1)} %maximum_select_fusion.1), channel_id=1, source_target_pairs={{0,16},{8,24},{16,0},{24,8},{1,17},{9,25},{17,1},{25,9},{2,18},{10... | collective-permute-start | bytes 245768 | tf_op jit(solution)/shard_map/ppermute | solution.py:183
  117.7 0.5 collective-permute-start.13
  118.3 0.6 collective-permute-done.11
  118.9 1.6 collective-permute-done.12
  120.5 0.8 collective-permute-done.13
  121.3 2.1 %collective-permute-start.14 = (bf16[640,256]{1,0:T(8,128)(2,1)S(1)}, bf16[640,256]{1,0:T(8,128)(2,1)S(1)}, u32[]{:S(2)}, u32[]{:S(2)}) collective-permute-start(bf16[640,256]{1,0:T(8,128)(2,1)S(1)} %bitcast.79), channel_id=1, source_target_pairs={{0,32},{32,128},{128,160},{160,0},{1,33},{33,129},{129,161},{161,1... | collective-permute-start | bytes 983048 | tf_op jit(solution)/shard_map/ppermute | solution.py:183
  123.4 3.4 %collective-permute-start.15 = (bf16[640,256]{1,0:T(8,128)(2,1)S(1)}, bf16[640,256]{1,0:T(8,128)(2,1)S(1)}, u32[]{:S(2)}, u32[]{:S(2)}) collective-permute-start(bf16[640,256]{1,0:T(8,128)(2,1)S(1)} %bitcast.80), channel_id=1, source_target_pairs={{0,128},{32,160},{128,0},{160,32},{1,129},{33,161},{129,1},{161,33... | collective-permute-start | bytes 983048 | tf_op jit(solution)/shard_map/ppermute | solution.py:183
  126.8 0.1 broadcast_in_dim.42
  126.9 3.2 %collective-permute-done.14 = bf16[640,256]{1,0:T(8,128)(2,1)S(1)} collective-permute-done((bf16[640,256]{1,0:T(8,128)(2,1)S(1)}, bf16[640,256]{1,0:T(8,128)(2,1)S(1)}, u32[]{:S(2)}, u32[]{:S(2)}) %collective-permute-start.14) | collective-permute-done | bytes 327712 | tf_op jit(solution)/shard_map/ppermute | solution.py:183
  130.1 4.7 %collective-permute-done.15 = bf16[640,256]{1,0:T(8,128)(2,1)S(1)} collective-permute-done((bf16[640,256]{1,0:T(8,128)(2,1)S(1)}, bf16[640,256]{1,0:T(8,128)(2,1)S(1)}, u32[]{:S(2)}, u32[]{:S(2)}) %collective-permute-start.15) | collective-permute-done | bytes 327712 | tf_op jit(solution)/shard_map/ppermute | solution.py:183
  134.9 8.4 %collective-permute-start.17 = (bf16[2560,256]{1,0:T(8,128)(2,1)S(1)}, bf16[2560,256]{1,0:T(8,128)(2,1)S(1)}, u32[]{:S(2)}, u32[]{:S(2)}) collective-permute-start(bf16[2560,256]{1,0:T(8,128)(2,1)S(1)} %bitcast.68), channel_id=1, source_target_pairs={{0,64},{64,0},{1,65},{65,1},{2,66},{66,2},{3,67},{67,3},{4,68},{68... | collective-permute-start | bytes 3932168 | tf_op jit(solution)/shard_map/ppermute | solution.py:162
  143.3 0.1 all_to_all.17
  143.4 15.3 %all_to_all.21 = f32[64,1,32]{2,1,0:T(1,128)S(1)} all-to-all(f32[64,1,32]{2,1,0:T(1,128)S(1)} %bitcast.88), channel_id=1, replica_groups=mesh['x_hi'=2,'core'=2,'x_lo'=2,'y'=4,'z'=8] {'x_lo','y','z'}, dimensions={0} | all-to-all | bytes 16384 | tf_op jit(solution)/shard_map/all_to_all | solution.py:279
  158.7 0.5 broadcast.31
  159.3 0.7 reduce.11
  160.0 0.7 reshape.135
  160.7 2.5 %shard_map.187 = (f32[256,256]{1,0:T(8,128)}, f32[1,256]{1,0:T(1,128)}, f32[3,256,512]{2,1,0:T(8,128)}, f32[512,256]{1,0:T(8,128)}, f32[1,256]{1,0:T(1,128)}, /*...) custom-call(s32[1]{0:T(128)} %bitcast.core_ref, ...), custom_call_target="tpu_custom_call" | custom-call | tf_op jit(solution)/shard_map/pallas_call | solution.py:233
  (33 shorter events, 0.4 us)
Async XLA Ops:
  4.7 20.7 %all-to-all-start = ((s32[64,1,64]{2,1,0:T(1,128)}), s32[64,1,64]{2,1,0:T(1,128)S(1)}, u32[]{:S(2)}, u32[]{:S(2)}) async-start(s32[64,1,64]{2,1,0:T(1,128)} %bitcast.2), calls=%async_computation | async-start | bytes 65536 | tf_op jit(solution)/shard_map/all_to_all | solution.py:261
  25.7 1.1 copy-start
  26.8 1.1 copy-start.1
  28.0 0.9 copy-start.2
  28.9 0.9 copy-start.3
  29.9 0.9 copy-start.4
  30.8 0.9 copy-start.5
  31.7 0.7 copy-start.6
  32.3 0.7 copy-start.7
  33.0 0.7 copy-start.8
  58.4 6.9 %collective-permute-start = (f32[2560,256]{1,0:T(8,128)S(1)}, f32[2560,256]{1,0:T(8,128)}, u32[]{:S(2)}, u32[]{:S(2)}) collective-permute-start(f32[2560,256]{1,0:T(8,128)S(1)} %slice_bitcast_fusion), channel_id=1, source_target_pairs={{0,64},{64,0},{1,65},{65,1},{2,66},{66,2},{3,67},{67,3},{4,68},{68... | collective-permute-start | bytes 7864328 | tf_op jit(solution)/shard_map/ppermute | solution.py:162
  69.2 10.3 %collective-permute-start.1 = (bf16[640,256]{1,0:T(8,128)(2,1)}, bf16[640,256]{1,0:T(8,128)(2,1)S(1)}, u32[]{:S(2)}, u32[]{:S(2)}) collective-permute-start(bf16[640,256]{1,0:T(8,128)(2,1)} %get-tuple-element.32), channel_id=1, source_target_pairs={{0,32},{32,128},{128,160},{160,0},{1,33},{33,129},{129,161},{161,1... | collective-permute-start | bytes 983048 | tf_op jit(solution)/shard_map/ppermute | solution.py:172
  69.6 17.2 %collective-permute-start.2 = (bf16[640,256]{1,0:T(8,128)(2,1)}, bf16[640,256]{1,0:T(8,128)(2,1)S(1)}, u32[]{:S(2)}, u32[]{:S(2)}) collective-permute-start(bf16[640,256]{1,0:T(8,128)(2,1)} %get-tuple-element.34), channel_id=1, source_target_pairs={{0,128},{32,160},{128,0},{160,32},{1,129},{33,161},{129,1},{161,33... | collective-permute-start | bytes 983048 | tf_op jit(solution)/shard_map/ppermute | solution.py:172
  72.1 15.4 %collective-permute-start.3 = (bf16[640,256]{1,0:T(8,128)(2,1)}, bf16[640,256]{1,0:T(8,128)(2,1)}, u32[]{:S(2)}, u32[]{:S(2)}) collective-permute-start(bf16[640,256]{1,0:T(8,128)(2,1)} %get-tuple-element.33), channel_id=1, source_target_pairs={{0,160},{32,0},{128,32},{160,128},{1,161},{33,1},{129,33},{161,129... | collective-permute-start | bytes 983048 | tf_op jit(solution)/shard_map/ppermute | solution.py:172
  79.5 7.3 %copy-start.9 = (bf16[640,256]{1,0:T(8,128)(2,1)}, bf16[640,256]{1,0:T(8,128)(2,1)S(1)}, u32[]{:S(2)}) copy-start(bf16[640,256]{1,0:T(8,128)(2,1)S(1)} %collective-permute-done.1) | copy-start | bytes 983044
  86.8 0.7 copy-start.10
  88.9 5.8 %collective-permute-start.4 = (bf16[160,256]{1,0:T(8,128)(2,1)S(1)}, bf16[160,256]{1,0:T(8,128)(2,1)S(1)}, u32[]{:S(2)}, u32[]{:S(2)}) collective-permute-start(bf16[160,256]{1,0:T(8,128)(2,1)S(1)} %get-tuple-element.35), channel_id=1, source_target_pairs={{0,8},{8,16},{16,24},{24,0},{1,9},{9,17},{17,25},{25,1},{2,10},{10... | collective-permute-start | bytes 245768 | tf_op jit(solution)/shard_map/ppermute | solution.py:172
  89.3 5.4 %collective-permute-start.5 = (bf16[160,256]{1,0:T(8,128)(2,1)S(1)}, bf16[160,256]{1,0:T(8,128)(2,1)S(1)}, u32[]{:S(2)}, u32[]{:S(2)}) collective-permute-start(bf16[160,256]{1,0:T(8,128)(2,1)S(1)} %get-tuple-element.37), channel_id=1, source_target_pairs={{0,16},{8,24},{16,0},{24,8},{1,17},{9,25},{17,1},{25,9},{2,18},{10... | collective-permute-start | bytes 245768 | tf_op jit(solution)/shard_map/ppermute | solution.py:172
  90.9 4.4 %collective-permute-start.6 = (bf16[160,256]{1,0:T(8,128)(2,1)S(1)}, bf16[160,256]{1,0:T(8,128)(2,1)S(1)}, u32[]{:S(2)}, u32[]{:S(2)}) collective-permute-start(bf16[160,256]{1,0:T(8,128)(2,1)S(1)} %get-tuple-element.36), channel_id=1, source_target_pairs={{0,24},{8,0},{16,8},{24,16},{1,25},{9,1},{17,9},{25,17},{2,26},{10... | collective-permute-start | bytes 245768 | tf_op jit(solution)/shard_map/ppermute | solution.py:172
  95.3 3.4 %collective-permute-start.7 = (f32[80,256]{1,0:T(8,128)S(1)}, f32[80,256]{1,0:T(8,128)S(1)}, u32[]{:S(2)}, u32[]{:S(2)}) collective-permute-start(f32[80,256]{1,0:T(8,128)S(1)} %dynamic-slice_bitcast_fusion), channel_id=1, source_target_pairs={{0,1},{1,0},{2,3},{3,2},{4,5},{5,4},{6,7},{7,6},{8,9},{9,8},{10,11... | collective-permute-start | bytes 245768 | tf_op jit(solution)/shard_map/ppermute | solution.py:162
  98.7 4.4 %collective-permute-start.8 = (f32[80,256]{1,0:T(8,128)S(1)}, f32[80,256]{1,0:T(8,128)S(1)}, u32[]{:S(2)}, u32[]{:S(2)}) collective-permute-start(f32[80,256]{1,0:T(8,128)S(1)} %bitcast_add_fusion.3), channel_id=1, source_target_pairs={{0,2},{1,3},{2,0},{3,1},{4,6},{5,7},{6,4},{7,5},{8,10},{9,11},{10,... | collective-permute-start | bytes 245768 | tf_op jit(solution)/shard_map/ppermute | solution.py:162
  103.1 8.0 %collective-permute-start.9 = (f32[80,256]{1,0:T(8,128)S(1)}, f32[80,256]{1,0:T(8,128)S(1)}, u32[]{:S(2)}, u32[]{:S(2)}) collective-permute-start(f32[80,256]{1,0:T(8,128)S(1)} %add.145), channel_id=1, source_target_pairs={{0,4},{1,5},{2,6},{3,7},{4,0},{5,1},{6,2},{7,3},{8,12},{9,13},{10,... | collective-permute-start | bytes 245768 | tf_op jit(solution)/shard_map/ppermute | solution.py:162
  111.2 3.2 %collective-permute-start.10 = (bf16[80,256]{1,0:T(8,128)(2,1)S(1)}, bf16[80,256]{1,0:T(8,128)(2,1)S(1)}, u32[]{:S(2)}, u32[]{:S(2)}) collective-permute-start(bf16[80,256]{1,0:T(8,128)(2,1)S(1)} %add_convert_fusion), channel_id=1, source_target_pairs={{0,1},{1,0},{2,3},{3,2},{4,5},{5,4},{6,7},{7,6},{8,9},{9,8},{10,11... | collective-permute-start | bytes 122888 | tf_op jit(solution)/shard_map/ppermute | solution.py:162
  114.3 4.6 %collective-permute-start.11 = (bf16[160,256]{1,0:T(8,128)(2,1)S(1)}, bf16[160,256]{1,0:T(8,128)(2,1)S(1)}, u32[]{:S(2)}, u32[]{:S(2)}) collective-permute-start(bf16[160,256]{1,0:T(8,128)(2,1)S(1)} %maximum_select_fusion.1), channel_id=1, source_target_pairs={{0,8},{8,16},{16,24},{24,0},{1,9},{9,17},{17,25},{25,1},{2,10},{10... | collective-permute-start | bytes 245768 | tf_op jit(solution)/shard_map/ppermute | solution.py:183
  115.7 4.8 %collective-permute-start.12 = (bf16[160,256]{1,0:T(8,128)(2,1)S(1)}, bf16[160,256]{1,0:T(8,128)(2,1)S(1)}, u32[]{:S(2)}, u32[]{:S(2)}) collective-permute-start(bf16[160,256]{1,0:T(8,128)(2,1)S(1)} %maximum_select_fusion.1), channel_id=1, source_target_pairs={{0,16},{8,24},{16,0},{24,8},{1,17},{9,25},{17,1},{25,9},{2,18},{10... | collective-permute-start | bytes 245768 | tf_op jit(solution)/shard_map/ppermute | solution.py:183
  117.7 3.6 %collective-permute-start.13 = (bf16[160,256]{1,0:T(8,128)(2,1)S(1)}, bf16[160,256]{1,0:T(8,128)(2,1)S(1)}, u32[]{:S(2)}, u32[]{:S(2)}) collective-permute-start(bf16[160,256]{1,0:T(8,128)(2,1)S(1)} %maximum_select_fusion.1), channel_id=1, source_target_pairs={{0,24},{8,0},{16,8},{24,16},{1,25},{9,1},{17,9},{25,17},{2,26},{10... | collective-permute-start | bytes 245768 | tf_op jit(solution)/shard_map/ppermute | solution.py:183
  121.3 8.8 %collective-permute-start.14 = (bf16[640,256]{1,0:T(8,128)(2,1)S(1)}, bf16[640,256]{1,0:T(8,128)(2,1)S(1)}, u32[]{:S(2)}, u32[]{:S(2)}) collective-permute-start(bf16[640,256]{1,0:T(8,128)(2,1)S(1)} %bitcast.79), channel_id=1, source_target_pairs={{0,32},{32,128},{128,160},{160,0},{1,33},{33,129},{129,161},{161,1... | collective-permute-start | bytes 983048 | tf_op jit(solution)/shard_map/ppermute | solution.py:183
  123.4 11.4 %collective-permute-start.15 = (bf16[640,256]{1,0:T(8,128)(2,1)S(1)}, bf16[640,256]{1,0:T(8,128)(2,1)S(1)}, u32[]{:S(2)}, u32[]{:S(2)}) collective-permute-start(bf16[640,256]{1,0:T(8,128)(2,1)S(1)} %bitcast.80), channel_id=1, source_target_pairs={{0,128},{32,160},{128,0},{160,32},{1,129},{33,161},{129,1},{161,33... | collective-permute-start | bytes 983048 | tf_op jit(solution)/shard_map/ppermute | solution.py:183
  126.8 8.0 %collective-permute-start.16 = (bf16[640,256]{1,0:T(8,128)(2,1)S(1)}, bf16[640,256]{1,0:T(8,128)(2,1)S(1)}, u32[]{:S(2)}, u32[]{:S(2)}) collective-permute-start(bf16[640,256]{1,0:T(8,128)(2,1)S(1)} %bitcast.81), channel_id=1, source_target_pairs={{0,160},{32,0},{128,32},{160,128},{1,161},{33,1},{129,33},{161,129... | collective-permute-start | bytes 983048 | tf_op jit(solution)/shard_map/ppermute | solution.py:183
  134.9 25.8 %collective-permute-start.17 = (bf16[2560,256]{1,0:T(8,128)(2,1)S(1)}, bf16[2560,256]{1,0:T(8,128)(2,1)S(1)}, u32[]{:S(2)}, u32[]{:S(2)}) collective-permute-start(bf16[2560,256]{1,0:T(8,128)(2,1)S(1)} %bitcast.68), channel_id=1, source_target_pairs={{0,64},{64,0},{1,65},{65,1},{2,66},{66,2},{3,67},{67,3},{4,68},{68... | collective-permute-start | bytes 3932168 | tf_op jit(solution)/shard_map/ppermute | solution.py:162
where the time goes:
time: 166 us; the launch traced here: 163 us
  waiting for transfers between devices  55.2 us (33%)
  starting transfers between devices  44 us (27%)
  Pallas kernels  25.3 us (15%)
  blocking collectives  15.3 us (9%)
  local copies, waits for them, and re-layouts  14.1 us (8%)
  other arithmetic  8.49 us (5%)
    pallas_call x1, Pallas kernels, compute(): pl.pallas_call(functools.partial(kernel, step, chunk, loss_scale), out_sh...  22.8 us
    ppermute x6, waiting for transfers between devices, swap(): return lax.ppermute(array, axis, [(i, i ^ mask) for i in range(count)])  19.2 us
    ppermute x6, waiting for transfers between devices, scatter_sum(): got = lax.ppermute(sent, axis, [(i, (i + k) % count) for i in range(count)])  16.5 us
    all_to_all x1, blocking collectives, local(): loss = lax.all_to_all(loss.reshape(shards, step), ctx, 0, 0, tiled=True)  15.3 us
    ppermute x6, starting transfers between devices, swap(): return lax.ppermute(array, axis, [(i, i ^ mask) for i in range(count)])  15 us
    all_to_all x1, starting transfers between devices, local(): both = lax.all_to_all(both, ctx, 0, 0, tiled=True)  12.1 us
    ppermute x6, waiting for transfers between devices, gather(): lax.ppermute(array, axis, [(i, (i + k) % count) for i in range(count)])  10.9 us
    ppermute x6, starting transfers between devices, gather(): lax.ppermute(array, axis, [(i, (i + k) % count) for i in range(count)])  9.35 us
  transfers between devices with their start and end apart: 19, of which 15 were waited for; matrix products, arithmetic and copies ran while one was open for 1% of the time, Pallas kernels for 0%

commit v1 on v0

v1 whole, which is shorter than its diff:
```python
import functools

import jax
import jax.numpy as jnp
from jax import lax
from jax.experimental import pallas as pl
from jax.experimental.pallas import tpu as pltpu
from jax.sharding import Mesh, PartitionSpec as P

EPS = 1e-05
BF = jnp.bfloat16
F32 = jnp.float32
WIDE = 256
LANES = 128
LEAD = 128
CHUNK = 1024
STEP = 32
PART = 40
TAPS_AT, OUT_AT, GAINS_AT = 512, 3584, 4608
X = ("x_hi", "x_lo")


def rows_dot(left, right):
    return lax.dot_general(left, right, (((0,), (0,)), ((), ())), preferred_element_type=F32)


def cols_dot(left, right):
    return lax.dot_general(left, right, (((1,), (1,)), ((), ())), preferred_element_type=F32)


def dot(left, right):
    return jnp.dot(left, right, preferred_element_type=F32)


def mean(values):
    return jnp.sum(values, axis=-1, keepdims=True) * (1.0 / WIDE)


def kernel(
    peers,
    loss_scale,
    both_ref,
    embed_hbm,
    gain1_hbm,
    taps1_hbm,
    out1_hbm,
    gain2_hbm,
    taps2_hbm,
    out2_hbm,
    gainf_hbm,
    head_hbm,
    loss_ref,
    *rest,
):
    part = peers * PART
    keep_refs, send_refs = rest[:4], rest[4:8]
    (embed_ref, gain1_ref, taps1_ref, out1_ref, gain2_ref, taps2_ref, out2_ref, gainf_ref, head_ref) = rest[8:17]
    (sems, tok_ref, targ_ref, hot_ref, x0_ref, h1_ref, a1_ref, x1_ref, h2_ref, a2_ref, gx2_ref, gc2_ref, gc1_ref) = rest[17:30]
    losses_ref, acc_ref = rest[30:]
    sources = (embed_hbm, gain1_hbm, taps1_hbm, out1_hbm, gain2_hbm, taps2_hbm, out2_hbm, gainf_hbm, head_hbm)
    copies = [pltpu.make_async_copy(src, dst, sems.at[i]) for i, (src, dst) in enumerate(zip(sources, rest[8:17]))]
    for copy in copies:
        copy.start()
    rows = x0_ref.shape[0]
    n = rows // CHUNK
    shards = CHUNK // STEP
    zeros = jnp.zeros((LEAD, WIDE), BF)
    h1_ref[0:LEAD, :] = zeros
    h2_ref[0:LEAD, :] = zeros
    gc1_ref[rows : rows + LEAD, :] = jnp.zeros((LEAD, 2 * WIDE), BF)
    gc2_ref[rows : rows + LEAD, :] = jnp.zeros((LEAD, 2 * WIDE), BF)
    acc_ref[...] = jnp.zeros_like(acc_ref)
    quarter = lax.rem(lax.axis_index("z"), 4)

    def mine(block):
        pieces = [block[:, STEP * p : STEP * (p + 1)] for p in range(4)]
        low = jnp.where(quarter == 0, pieces[0], pieces[1])
        high = jnp.where(quarter == 2, pieces[2], pieces[3])
        return jnp.where(quarter < 2, low, high)

    tok_ref[...] = mine(both_ref[:, 0, :])
    targ_ref[...] = mine(both_ref[:, 1, :])
    letters = lax.broadcasted_iota(jnp.int32, (CHUNK, WIDE), 1)
    diagonal = lax.rem(lax.broadcasted_iota(jnp.int32, (CHUNK, STEP), 0), STEP) == lax.broadcasted_iota(
        jnp.int32, (CHUNK, STEP), 1
    )

    def column(ref, i):
        block = ref[pl.ds(pl.multiple_of(i * shards, shards), shards), :]
        tall = jnp.broadcast_to(block[:, None, :], (shards, STEP, STEP)).reshape(CHUNK, STEP)
        return jnp.sum(jnp.where(diagonal, tall, 0), axis=1, keepdims=True)

    def add(half, at, value):
        height = value.shape[0]
        for b in range(value.shape[1] // LANES):
            start = at + b * height
            acc_ref[half, start : start + height, :] += value[:, b * LANES : (b + 1) * LANES]

    for copy in copies:
        copy.wait()

    def forward(i, carry):
        t0 = pl.multiple_of(i * CHUNK, CHUNK)
        here = pl.ds(t0, CHUNK)
        onehot = (column(tok_ref, i) == letters).astype(F32).astype(BF)
        hot_ref[here, :] = onehot
        x0 = dot(onehot, embed_ref[...])
        x0_ref[here, :] = x0.astype(BF)

        def layer(x, gain_ref, taps_ref, out_ref, h_ref, a_ref, dist):
            s = lax.rsqrt(mean(x * x) + EPS)
            h = jnp.maximum(x * s * gain_ref[...], 0.0).astype(BF)
            h_ref[pl.ds(t0 + LEAD, CHUNK), :] = h
            near = h_ref[pl.ds(t0 + LEAD - dist, CHUNK), :]
            far = h_ref[pl.ds(t0 + LEAD - 2 * dist, CHUNK), :]
            a = jnp.maximum(dot(jnp.concatenate([h, near, far], axis=1), taps_ref[...]), 0.0).astype(BF)
            a_ref[here, :] = a
            return x + dot(a, out_ref[...]), a

        x1, _ = layer(x0, gain1_ref, taps1_ref, out1_ref, h1_ref, a1_ref, STEP)
        x1_ref[here, :] = x1
        x2, a = layer(x1, gain2_ref, taps2_ref, out2_ref, h2_ref, a2_ref, 2 * STEP)
        s = lax.rsqrt(mean(x2 * x2) + EPS)
        normed = x2 * s
        final = (normed * gainf_ref[...]).astype(BF)
        logits = dot(final, head_ref[...])
        highest = jnp.max(logits, axis=1, keepdims=True)
        e = jnp.exp(logits - highest)
        total = jnp.sum(e, axis=1, keepdims=True)
        wanted = (column(targ_ref, i) == letters).astype(F32)
        loss = highest + jnp.log(total) - jnp.sum(logits * wanted, axis=1, keepdims=True)
        spread = jnp.where(diagonal, loss, 0.0).reshape(shards, STEP, STEP)
        losses_ref[pl.ds(pl.multiple_of(i * shards, shards), shards), :] = jnp.sum(spread, axis=1)
        gl = ((e * (1.0 / total) - wanted) * loss_scale).astype(BF)
        add(1, 0, rows_dot(final, gl))
        gfin = cols_dot(gl, head_ref[...])
        add(1, GAINS_AT + 2, jnp.sum(gfin * normed, axis=0, keepdims=True))
        w = gfin * gainf_ref[...]
        gx2 = s * (w - normed * mean(w * normed))
        gx2_ref[here, :] = gx2
        low = gx2.astype(BF)
        add(1, OUT_AT, rows_dot(a, low))
        gact = cols_dot(low, out2_ref[...])
        gc2_ref[here, :] = jnp.where(a > 0, gact, 0.0).astype(BF)
        return carry

    lax.fori_loop(0, n, forward, 0)

    losses = losses_ref[...]
    high = losses.astype(BF).astype(F32)
    low = losses - high
    half = peers
    loss_ref[...] = jnp.concatenate([high[:half], low[:half], high[half:], low[half:]], axis=1).astype(BF)

    def back(i, carry):
        j = n - 1 - i
        t0 = pl.multiple_of(j * CHUNK, CHUNK)
        here = pl.ds(t0, CHUNK)

        def block(g, x, h, gc_ref, half, taps_ref, gain, dist):
            gcs = [gc_ref[pl.ds(t0 + k * dist, CHUNK), :] for k in range(3)]
            gh = sum(cols_dot(gcs[k], taps_ref[k * WIDE : (k + 1) * WIDE, :]) for k in range(3))
            for k in range(3):
                add(half, TAPS_AT + 1024 * k, rows_dot(h, gcs[k]))
            gn = jnp.where(h > 0, gh, 0.0)
            s = lax.rsqrt(mean(x * x) + EPS)
            normed = x * s
            add(half, GAINS_AT, jnp.sum(gn * normed, axis=0, keepdims=True))
            w = gn * gain
            return g + s * (w - normed * mean(w * normed))

        h2 = h2_ref[pl.ds(t0 + LEAD, CHUNK), :]
        gx1 = block(gx2_ref[here, :], x1_ref[here, :], h2, gc2_ref, 1, taps2_ref, gain2_ref[...], 2 * STEP)
        low = gx1.astype(BF)
        a = a1_ref[here, :]
        add(0, OUT_AT, rows_dot(a, low))
        gact = cols_dot(low, out1_ref[...])
        gc1_ref[here, :] = jnp.where(a > 0, gact, 0.0).astype(BF)
        h1 = h1_ref[pl.ds(t0 + LEAD, CHUNK), :]
        gx0 = block(gx1, x0_ref[here, :].astype(F32), h1, gc1_ref, 0, taps1_ref, gain1_ref[...], STEP)
        add(0, 0, rows_dot(hot_ref[here, :], gx0.astype(BF)))
        return carry

    lax.fori_loop(0, n, back, 0)

    core, x = lax.axis_index("core"), lax.axis_index(X)
    for k in range(4):
        at = pl.ds(pl.multiple_of(lax.rem(x + k, 4) * part, part), part)
        keep_refs[k][...] = acc_ref[core, at, :]
        send_refs[k][...] = acc_ref[1 - core, at, :]


def compute(both, weights, loss_scale, peers):
    rows = both.shape[0] * STEP
    part = peers * PART
    vmem, hbm = pl.BlockSpec(memory_space=pltpu.VMEM), pl.BlockSpec(memory_space=pltpu.HBM)
    shapes = [(WIDE, BF), (2 * WIDE, BF), (WIDE, F32)]
    tall = lambda wide, dtype, extra=0: pltpu.VMEM((rows + extra, wide), dtype)
    return pl.pallas_call(
        functools.partial(kernel, peers, loss_scale),
        out_shape=[jax.ShapeDtypeStruct((peers, LANES), BF)] + [jax.ShapeDtypeStruct((part, LANES), F32)] * 8,
        in_specs=[vmem] + [hbm] * len(weights),
        out_specs=[vmem] * 9,
        scratch_shapes=[pltpu.VMEM(w.shape, w.dtype) for w in weights]
        + [
            pltpu.SemaphoreType.DMA((len(weights),)),
            pltpu.VMEM((rows // STEP, STEP), jnp.int32),
            pltpu.VMEM((rows // STEP, STEP), jnp.int32),
            tall(WIDE, BF),
            tall(WIDE, BF),
            tall(WIDE, BF, LEAD),
            tall(2 * WIDE, BF),
            tall(WIDE, F32),
            tall(WIDE, BF, LEAD),
            tall(2 * WIDE, BF),
            tall(WIDE, F32),
            tall(2 * WIDE, BF, LEAD),
            tall(2 * WIDE, BF, LEAD),
            pltpu.VMEM((rows // STEP, STEP), F32),
            pltpu.VMEM((2, 4 * part, LANES), F32),
        ],
        compiler_params=pltpu.CompilerParams(vmem_limit_bytes=57 * 2**20),
    )(both, *weights)


def swap(array, axis, mask):
    count = lax.axis_size(axis)
    return lax.ppermute(array, axis, [(i, i ^ mask) for i in range(count)])


def shift(array, axis, by):
    count = lax.axis_size(axis)
    return lax.ppermute(array, axis, [(i, (i + by) % count) for i in range(count)])


def reduce_all(keep, send, loss):
    parts = [mine + swap(other, "core", 1) for mine, other in zip(keep, send)]
    total = parts[0]
    for k in range(1, 4):
        total = total + shift(parts[k].astype(BF), X, k).astype(F32)
    rest = ("y", "z")
    peers = lax.axis_size(rest)
    message = total.astype(BF).reshape(peers, PART, LANES)
    message = jnp.concatenate([message, jnp.broadcast_to(loss[:, None], (peers, 8, LANES))], axis=1)
    got = lax.all_to_all(message, rest, 0, 0, tiled=True)
    loss = got[:, PART]
    summed = jnp.sum(got[:, :PART].astype(F32), axis=0).astype(BF)
    whole = jnp.broadcast_to(summed[None], (peers, PART, LANES))
    whole = lax.all_to_all(whole, rest, 0, 0, tiled=True).reshape(-1, LANES)
    mine = [whole] + [shift(whole, X, k) for k in range(1, 4)]
    return mine, [swap(piece, "core", 1) for piece in mine], loss, swap(loss, "x_lo", 1)


def spread_kernel(*refs):
    mine, others = refs[:4], refs[4:8]
    loss_mine, loss_other = refs[8:10]
    loss_ref, embed, gain1, taps1, out1, gain2, taps2, out2, gainf, head = refs[10:20]
    big, lines = refs[20:]
    core, x, x_lo = lax.axis_index("core"), lax.axis_index(X), lax.axis_index("x_lo")
    part = mine[0].shape[0]
    for k in range(4):
        at = pl.ds(pl.multiple_of(lax.rem(x + 4 - k, 4) * part, part), part)
        big[core, at, :] = mine[k][...]
        big[1 - core, at, :] = others[k][...]

    def write(half, square, taps, out_w, gains):
        def put(target, at, height, count):
            for b in range(count):
                start = at + b * height
                target[:, b * LANES : (b + 1) * LANES] = big[half, start : start + height, :].astype(F32)

        put(square, 0, 256, 2)
        for k in range(3):
            put(taps.at[k], TAPS_AT + 1024 * k, 256, 4)
        put(out_w, OUT_AT, 512, 2)
        tail = big[half, GAINS_AT : GAINS_AT + 16, :].astype(F32)
        for i, gain in enumerate(gains):
            gain[:, :LANES] = tail[2 * i : 2 * i + 1]
            gain[:, LANES:] = tail[2 * i + 1 : 2 * i + 2]

    write(0, embed, taps1, out1, [gain1])
    write(1, head, taps2, out2, [gain2, gainf])

    def joined(ref):
        block = ref[...].astype(F32)
        first = block[:, :STEP] + block[:, STEP : 2 * STEP]
        second = block[:, 2 * STEP : 3 * STEP] + block[:, 3 * STEP :]
        return jnp.where(x_lo == 0, first, second)

    here, there = joined(loss_mine), joined(loss_other)
    half = here.shape[0]
    lines[:half, :] = jnp.where(x_lo == 0, here, there)
    lines[half:, :] = jnp.where(x_lo == 0, there, here)
    for b in range(4):
        loss_ref[:, b * STEP : (b + 1) * STEP] = lines[pl.ds(b, half // 2, stride=4), :]


def spread(mine, others, loss_mine, loss_other):
    vmem = pl.BlockSpec(memory_space=pltpu.VMEM)
    part = mine[0].shape[0]
    peers = loss_mine.shape[0]
    square, taps, out_w, gain = (256, 256), (3, 256, 512), (512, 256), (1, 256)
    shapes = [(peers // 2, LANES), square, gain, taps, out_w, gain, taps, out_w, gain, square]
    return pl.pallas_call(
        spread_kernel,
        out_shape=[jax.ShapeDtypeStruct(s, F32) for s in shapes],
        in_specs=[vmem] * 10,
        out_specs=[vmem] * len(shapes),
        scratch_shapes=[pltpu.VMEM((2, 4 * part, LANES), BF), pltpu.VMEM((2 * peers, STEP), F32)],
        compiler_params=pltpu.CompilerParams(vmem_limit_bytes=32 * 2**20),
    )(*mine, *others, loss_mine, loss_other)


def local(tokens, targets, embed, gain1, taps1, out1, gain2, taps2, out2, gainf, head):
    ctx = ("x_lo", "y", "z")
    count = tokens.shape[1]
    shards = lax.axis_size(ctx)
    loss_scale = float(count * shards * lax.axis_size(("x_hi", "core"))) ** (-0.5)
    lines = jnp.stack([tokens.reshape(-1, LANES), targets.reshape(-1, LANES)], axis=1)
    both = jnp.broadcast_to(lines[:, None], (lines.shape[0], 4, 2, LANES)).reshape(shards, 2, LANES)
    both = lax.all_to_all(both, ctx, 0, 0, tiled=True)
    weights = (
        embed,
        gain1[None],
        taps1.reshape(-1, 512),
        out1,
        gain2[None],
        taps2.reshape(-1, 512),
        out2,
        gainf[None],
        head,
    )
    outs = compute(both, weights, loss_scale, shards // 2)
    mine, others, loss_mine, loss_other = reduce_all(outs[1:5], outs[5:9], outs[0])
    loss, *grads = spread(mine, others, loss_mine, loss_other)
    for i in (1, 4, 7):
        grads[i] = grads[i][0]
    return (loss.reshape(1, count), *grads)


def solution(mesh):
    fine = Mesh(mesh.devices.reshape(2, 2, 2, 4, 8), ("x_hi", "core", "x_lo", "y", "z"))
    data = P(("x_hi", "core"), ("x_lo", "y", "z"))
    in_specs = (data, data, P(), P(), P(), P(), P(), P(), P(), P(), P())
    out_specs = (data, P(), P(), P(), P(), P(), P(), P(), P(), P())
    return jax.shard_map(local, mesh=fine, in_specs=in_specs, out_specs=out_specs, check_vma=False)
```

time: 166 us -> 135 us (0.81); the launches traced: 163 us -> 135 us
  blocking collectives: 15.3 us -> 53.6 us
  waiting for transfers between devices: 55.2 us -> 21.7 us
  starting transfers between devices: 44 us -> 27.6 us
  local copies, waits for them, and re-layouts: 14.1 us -> 0.12 us
  other arithmetic: 8.49 us -> 2.35 us
  Pallas kernels: 25.3 us -> 28.4 us
    all_to_all x1 -> x3, blocking collectives: 15.3 us -> 53.6 us  [the longest x1 21.2 us: local(): both = lax.all_to_all(both, ctx, 0, 0, tiled=True)]
    ppermute x6 -> x9, waiting for transfers between devices: 19.2 us -> 3.65 us  [swap(): return lax.ppermute(array, axis, [(i, i ^ mask) for i in range(count)])]
    all_to_all x1 -> x0, starting transfers between devices: 12.1 us -> none  [local(): both = lax.all_to_all(both, ctx, 0, 0, tiled=True)]
    ppermute x12 -> x6, waiting for transfers between devices: 27.3 us -> 18 us  [shift(): lax.ppermute(array, axis, [(i, (i + by) % count) for i in range(count)])]
    unnamed x23 -> x9, local copies, waits for them, and re-layouts: 9.26 us -> 0.02 us
    all_to_all x1 -> x0, waiting for transfers between devices: 8.58 us -> none  [local(): both = lax.all_to_all(both, ctx, 0, 0, tiled=True)]
    ppermute x12 -> x6, starting transfers between devices: 16.8 us -> 12.1 us  [shift(): lax.ppermute(array, axis, [(i, (i + by) % count) for i in range(count)])]
    add x5 -> x0, other arithmetic: 4.28 us -> none  [the longest x1 2.87 us: reduce_all(): total = keep + swap(send, 'core', 1)]
  transfers between devices with their start and end apart: 19 -> 15, of which waited for: 15 -> 7; matrix products, arithmetic and copies ran while one was open for 1% -> 1% of each run, Pallas kernels for 0% -> 0%
where the time goes in v1:
time: 135 us
  blocking collectives  53.6 us (40%)
  Pallas kernels  28.4 us (21%)
  starting transfers between devices  27.6 us (20%)
  waiting for transfers between devices  21.7 us (16%)
  other arithmetic  2.35 us (2%)
    pallas_call x1, Pallas kernels, compute(): pl.pallas_call(functools.partial(kernel, peers, loss_scale), out_shape=[j...  25.8 us
    all_to_all x1, blocking collectives, local(): both = lax.all_to_all(both, ctx, 0, 0, tiled=True)  21.2 us
    ppermute x6, waiting for transfers between devices, shift(): lax.ppermute(array, axis, [(i, (i + by) % count) for i in range(count)])  18 us
    all_to_all x1, blocking collectives, reduce_all(): got = lax.all_to_all(message, rest, 0, 0, tiled=True)  17.5 us
    ppermute x9, starting transfers between devices, swap(): return lax.ppermute(array, axis, [(i, i ^ mask) for i in range(count)])  15.5 us
    all_to_all x1, blocking collectives, reduce_all(): whole = lax.all_to_all(whole, rest, 0, 0, tiled=True).reshape(-1, LANES)  15 us
    ppermute x6, starting transfers between devices, shift(): lax.ppermute(array, axis, [(i, (i + by) % count) for i in range(count)])  12.1 us
    ppermute x9, waiting for transfers between devices, swap(): return lax.ppermute(array, axis, [(i, i ^ mask) for i in range(count)])  3.65 us
  transfers between devices with their start and end apart: 15, of which 7 were waited for; matrix products, arithmetic and copies ran while one was open for 1% of the time, Pallas kernels for 0%

profile of v1, /device:TPU:33, one launch (start us, length us, event | category | flops | bytes accessed | tf_op | source)
XLA Modules:
  0.0 134.6 jit_solution(18106155140593101262)
XLA Ops:
  0.6 0.7 pad_add_fusion
  1.4 21.2 %all_to_all.15.both_ref = s32[64,2,128]{2,1,0:T(2,128)} all-to-all(s32[64,2,128]{2,1,0:T(2,128)S(1)} %bitcast.27), channel_id=1, replica_groups=mesh['x_hi'=2,'core'=2,'x_lo'=2,'y'=4,'z'=8] {'x_lo','y','z'}, dimensions={0} | all-to-all | bytes 131072 | tf_op jit(solution)/shard_map/all_to_all | solution.py:321
  22.6 25.8 %shard_map.186 = (bf16[32,128]{1,0:T(8,128)(2,1)}, f32[1280,128]{1,0:T(8,128)}, f32[1280,128]{1,0:T(8,128)}, f32[1280,128]{1,0:T(8,128)}, f32[1280,128]{1,0:T(8,...) custom-call(s32[64,2,128]{2,1,0:T(2,128)} %all_to_all.15.both_ref, ...), custom_call_target="tpu_custom_call" | custom-call | tf_op jit(solution)/shard_map/pallas_call | solution.py:199
  48.4 0.0 copy-start.2
  48.4 2.0 %collective-permute-start.1 = (f32[1280,128]{1,0:T(8,128)}, f32[1280,128]{1,0:T(8,128)S(1)}, u32[]{:S(2)}, u32[]{:S(2)}) collective-permute-start(f32[1280,128]{1,0:T(8,128)} %get-tuple-element.32), channel_id=1, source_target_pairs={{0,64},{64,0},{1,65},{65,1},{2,66},{66,2},{3,67},{67,3},{4,68},{68... | collective-permute-start | bytes 1966088 | tf_op jit(solution)/shard_map/ppermute | solution.py:228
  50.4 0.3 collective-permute-start.3
  50.7 0.2 collective-permute-start
  50.9 0.3 collective-permute-start.5
  51.2 1.1 collective-permute-done.1
  52.3 0.0 copy-start.1
  52.3 1.2 add_convert_fusion.3
  53.5 0.7 collective-permute-start.2
  54.2 0.0 collective-permute-done.3
  54.2 0.0 copy-done.2
  54.2 0.0 copy-start
  54.2 0.1 add_convert_fusion.2
  54.3 2.5 %collective-permute-start.4 = (bf16[1280,128]{1,0:T(8,128)(2,1)S(1)}, bf16[1280,128]{1,0:T(8,128)(2,1)S(1)}, u32[]{:S(2)}, u32[]{:S(2)}) collective-permute-start(bf16[1280,128]{1,0:T(8,128)(2,1)S(1)} %add_convert_fusion.2), channel_id=1, source_target_pairs={{0,128},{32,160},{128,0},{160,32},{1,129},{33,161},{129,1},{161,33... | collective-permute-start | bytes 983048 | tf_op jit(solution)/shard_map/ppermute | solution.py:233
  56.8 0.0 collective-permute-done.5
  56.8 0.0 copy-done.1
  56.8 0.1 add_convert_fusion.1
  56.9 0.0 copy-start.3
  56.9 1.6 %collective-permute-start.6 = (bf16[1280,128]{1,0:T(8,128)(2,1)S(1)}, bf16[1280,128]{1,0:T(8,128)(2,1)S(1)}, u32[]{:S(2)}, u32[]{:S(2)}) collective-permute-start(bf16[1280,128]{1,0:T(8,128)(2,1)S(1)} %add_convert_fusion.1), channel_id=1, source_target_pairs={{0,160},{32,0},{128,32},{160,128},{1,161},{33,1},{129,33},{161,129... | collective-permute-start | bytes 983048 | tf_op jit(solution)/shard_map/ppermute | solution.py:233
  58.5 0.0 collective-permute-done
  58.5 5.3 %collective-permute-done.2 = bf16[1280,128]{1,0:T(8,128)(2,1)S(1)} collective-permute-done((bf16[1280,128]{1,0:T(8,128)(2,1)S(1)}, bf16[1280,128]{1,0:T(8,128)(2,1)S(1)}, u32[]{:S(2)}, u32[]{:S(2)}) %collective-permute-start.2) | collective-permute-done | bytes 327712 | tf_op jit(solution)/shard_map/ppermute | solution.py:233
  63.8 7.4 %collective-permute-done.4 = bf16[1280,128]{1,0:T(8,128)(2,1)S(1)} collective-permute-done((bf16[1280,128]{1,0:T(8,128)(2,1)S(1)}, bf16[1280,128]{1,0:T(8,128)(2,1)S(1)}, u32[]{:S(2)}, u32[]{:S(2)}) %collective-permute-start.4) | collective-permute-done | bytes 327712 | tf_op jit(solution)/shard_map/ppermute | solution.py:233
  71.1 0.1 collective-permute-done.6
  71.2 0.0 copy-done
  71.2 0.2 add_convert_fusion
  71.4 0.0 copy-done.3
  71.5 17.5 %all_to_all.16 = bf16[32,48,128]{2,1,0:T(8,128)(2,1)S(1)} all-to-all(bf16[32,48,128]{2,1,0:T(8,128)(2,1)S(1)} %pad_maximum_fusion), channel_id=1, replica_groups=mesh['x_hi'=2,'core'=2,'x_lo'=2,'y'=4,'z'=8] {'y','z'}, dimensions={0} | all-to-all | bytes 786432 | tf_op jit(solution)/shard_map/all_to_all | solution.py:245
  89.0 0.1 slice_reduce_fusion
  89.1 15.0 %all_to_all.17 = bf16[32,40,128]{2,1,0:T(8,128)(2,1)S(1)} all-to-all(bf16[32,40,128]{2,1,0:T(8,128)(2,1)S(1)} %broadcast_in_dim.32), channel_id=1, replica_groups=mesh['x_hi'=2,'core'=2,'x_lo'=2,'y'=4,'z'=8] {'y','z'}, dimensions={0} | all-to-all | bytes 655360 | tf_op jit(solution)/shard_map/all_to_all | solution.py:249
  104.1 6.6 %collective-permute-start.9 = (bf16[1280,128]{1,0:T(8,128)(2,1)S(1)}, bf16[1280,128]{1,0:T(8,128)(2,1)S(1)}, u32[]{:S(2)}, u32[]{:S(2)}) collective-permute-start(bf16[1280,128]{1,0:T(8,128)(2,1)S(1)} %bitcast.17), channel_id=1, source_target_pairs={{0,160},{32,0},{128,32},{160,128},{1,161},{33,1},{129,33},{161,129... | collective-permute-start | bytes 983048 | tf_op jit(solution)/shard_map/ppermute | solution.py:233
  110.7 0.7 collective-permute-start.8
  111.4 0.0 collective-permute-start.7
  111.4 2.7 %collective-permute-start.10 = (bf16[1280,128]{1,0:T(8,128)(2,1)S(1)}, bf16[1280,128]{1,0:T(8,128)(2,1)S(1)}, u32[]{:S(2)}, u32[]{:S(2)}) collective-permute-start(bf16[1280,128]{1,0:T(8,128)(2,1)S(1)} %bitcast.20), channel_id=1, source_target_pairs={{0,64},{64,0},{1,65},{65,1},{2,66},{66,2},{3,67},{67,3},{4,68},{68... | collective-permute-start | bytes 983048 | tf_op jit(solution)/shard_map/ppermute | solution.py:228
  114.1 2.1 %collective-permute-done.9.refs_3_ = bf16[1280,128]{1,0:T(8,128)(2,1)S(1)} collective-permute-done((bf16[1280,128]{1,0:T(8,128)(2,1)S(1)}, bf16[1280,128]{1,0:T(8,128)(2,1)S(1)}, u32[]{:S(2)}, u32[]{:S(2)}) %collective-permute-start.9) | collective-permute-done | bytes 327712 | tf_op jit(solution)/shard_map/ppermute | solution.py:233
  116.2 9.4 %collective-permute-start.13 = (bf16[1280,128]{1,0:T(8,128)(2,1)S(1)}, bf16[1280,128]{1,0:T(8,128)(2,1)S(1)}, u32[]{:S(2)}, u32[]{:S(2)}) collective-permute-start(bf16[1280,128]{1,0:T(8,128)(2,1)S(1)} %collective-permute-done.9.refs_3_), channel_id=1, source_target_pairs={{0,64},{64,0},{1,65},{65,1},{2,66},{66,2},{3,67},{67,3},{4,68},{68... | collective-permute-start | bytes 983048 | tf_op jit(solution)/shard_map/ppermute | solution.py:228
  125.6 0.0 collective-permute-done.8.refs_2_
  125.6 0.0 collective-permute-start.12
  125.6 3.2 %collective-permute-done.7.refs_1_ = bf16[1280,128]{1,0:T(8,128)(2,1)S(1)} collective-permute-done((bf16[1280,128]{1,0:T(8,128)(2,1)S(1)}, bf16[1280,128]{1,0:T(8,128)(2,1)S(1)}, u32[]{:S(2)}, u32[]{:S(2)}) %collective-permute-start.7) | collective-permute-done | bytes 327712 | tf_op jit(solution)/shard_map/ppermute | solution.py:233
  128.8 0.5 collective-permute-start.11
  129.4 0.1 collective-permute-start.14
  129.5 2.5 %collective-permute-done.14.refs_9_ = bf16[32,128]{1,0:T(8,128)(2,1)S(1)} collective-permute-done((bf16[32,128]{1,0:T(8,128)(2,1)S(1)}, bf16[32,128]{1,0:T(8,128)(2,1)S(1)}, u32[]{:S(2)}, u32[]{:S(2)}) %collective-permute-start.14) | collective-permute-done | bytes 8224 | tf_op jit(solution)/shard_map/ppermute | solution.py:228
  131.9 0.0 collective-permute-done.10.refs_4_
  131.9 0.0 collective-permute-done.13.refs_7_
  131.9 0.0 collective-permute-done.12.refs_6_
  132.0 0.0 collective-permute-done.11.refs_5_
  132.0 2.6 %shard_map.187 = (f32[16,128]{1,0:T(8,128)}, f32[256,256]{1,0:T(8,128)}, f32[1,256]{1,0:T(1,128)}, f32[3,256,512]{2,1,0:T(8,128)}, f32[512,256]{1,0:T(8,128)}, /...) custom-call(bf16[1280,128]{1,0:T(8,128)(2,1)S(1)} %bitcast.21, ...), custom_call_target="tpu_custom_call" | custom-call | tf_op jit(solution)/shard_map/pallas_call | solution.py:304
  (7 shorter events, 0.2 us)
Async XLA Ops:
  48.4 5.8 %copy-start.2 = (f32[1280,128]{1,0:T(8,128)S(1)}, f32[1280,128]{1,0:T(8,128)}, u32[]{:S(2)}) copy-start(f32[1280,128]{1,0:T(8,128)} %get-tuple-element.33) | copy-start | bytes 1966084
  48.4 3.9 %collective-permute-start.1 = (f32[1280,128]{1,0:T(8,128)}, f32[1280,128]{1,0:T(8,128)S(1)}, u32[]{:S(2)}, u32[]{:S(2)}) collective-permute-start(f32[1280,128]{1,0:T(8,128)} %get-tuple-element.32), channel_id=1, source_target_pairs={{0,64},{64,0},{1,65},{65,1},{2,66},{66,2},{3,67},{67,3},{4,68},{68... | collective-permute-start | bytes 1966088 | tf_op jit(solution)/shard_map/ppermute | solution.py:228
  50.4 3.8 %collective-permute-start.3 = (f32[1280,128]{1,0:T(8,128)}, f32[1280,128]{1,0:T(8,128)S(1)}, u32[]{:S(2)}, u32[]{:S(2)}) collective-permute-start(f32[1280,128]{1,0:T(8,128)} %get-tuple-element.34), channel_id=1, source_target_pairs={{0,64},{64,0},{1,65},{65,1},{2,66},{66,2},{3,67},{67,3},{4,68},{68... | collective-permute-start | bytes 1966088 | tf_op jit(solution)/shard_map/ppermute | solution.py:228
  50.7 7.8 %collective-permute-start = (f32[1280,128]{1,0:T(8,128)}, f32[1280,128]{1,0:T(8,128)S(1)}, u32[]{:S(2)}, u32[]{:S(2)}) collective-permute-start(f32[1280,128]{1,0:T(8,128)} %get-tuple-element.30), channel_id=1, source_target_pairs={{0,64},{64,0},{1,65},{65,1},{2,66},{66,2},{3,67},{67,3},{4,68},{68... | collective-permute-start | bytes 1966088 | tf_op jit(solution)/shard_map/ppermute | solution.py:228
  50.9 5.9 %collective-permute-start.5 = (f32[1280,128]{1,0:T(8,128)}, f32[1280,128]{1,0:T(8,128)S(1)}, u32[]{:S(2)}, u32[]{:S(2)}) collective-permute-start(f32[1280,128]{1,0:T(8,128)} %get-tuple-element.36), channel_id=1, source_target_pairs={{0,64},{64,0},{1,65},{65,1},{2,66},{66,2},{3,67},{67,3},{4,68},{68... | collective-permute-start | bytes 1966088 | tf_op jit(solution)/shard_map/ppermute | solution.py:228
  52.3 4.5 %copy-start.1 = (f32[1280,128]{1,0:T(8,128)S(1)}, f32[1280,128]{1,0:T(8,128)}, u32[]{:S(2)}) copy-start(f32[1280,128]{1,0:T(8,128)} %get-tuple-element.35) | copy-start | bytes 1966084
  53.5 10.2 %collective-permute-start.2 = (bf16[1280,128]{1,0:T(8,128)(2,1)S(1)}, bf16[1280,128]{1,0:T(8,128)(2,1)S(1)}, u32[]{:S(2)}, u32[]{:S(2)}) collective-permute-start(bf16[1280,128]{1,0:T(8,128)(2,1)S(1)} %add_convert_fusion.3), channel_id=1, source_target_pairs={{0,32},{32,128},{128,160},{160,0},{1,33},{33,129},{129,161},{161,1... | collective-permute-start | bytes 983048 | tf_op jit(solution)/shard_map/ppermute | solution.py:233
  54.2 17.0 %copy-start = (f32[1280,128]{1,0:T(8,128)S(1)}, f32[1280,128]{1,0:T(8,128)}, u32[]{:S(2)}) copy-start(f32[1280,128]{1,0:T(8,128)} %get-tuple-element.29) | copy-start | bytes 1966084
  54.3 16.8 %collective-permute-start.4 = (bf16[1280,128]{1,0:T(8,128)(2,1)S(1)}, bf16[1280,128]{1,0:T(8,128)(2,1)S(1)}, u32[]{:S(2)}, u32[]{:S(2)}) collective-permute-start(bf16[1280,128]{1,0:T(8,128)(2,1)S(1)} %add_convert_fusion.2), channel_id=1, source_target_pairs={{0,128},{32,160},{128,0},{160,32},{1,129},{33,161},{129,1},{161,33... | collective-permute-start | bytes 983048 | tf_op jit(solution)/shard_map/ppermute | solution.py:233
  56.9 14.5 %copy-start.3 = (bf16[32,128]{1,0:T(8,128)(2,1)S(1)}, bf16[32,128]{1,0:T(8,128)(2,1)}, u32[]{:S(2)}) copy-start(bf16[32,128]{1,0:T(8,128)(2,1)} %get-tuple-element.37) | copy-start | bytes 24580
  56.9 14.3 %collective-permute-start.6 = (bf16[1280,128]{1,0:T(8,128)(2,1)S(1)}, bf16[1280,128]{1,0:T(8,128)(2,1)S(1)}, u32[]{:S(2)}, u32[]{:S(2)}) collective-permute-start(bf16[1280,128]{1,0:T(8,128)(2,1)S(1)} %add_convert_fusion.1), channel_id=1, source_target_pairs={{0,160},{32,0},{128,32},{160,128},{1,161},{33,1},{129,33},{161,129... | collective-permute-start | bytes 983048 | tf_op jit(solution)/shard_map/ppermute | solution.py:233
  104.1 12.1 %collective-permute-start.9 = (bf16[1280,128]{1,0:T(8,128)(2,1)S(1)}, bf16[1280,128]{1,0:T(8,128)(2,1)S(1)}, u32[]{:S(2)}, u32[]{:S(2)}) collective-permute-start(bf16[1280,128]{1,0:T(8,128)(2,1)S(1)} %bitcast.17), channel_id=1, source_target_pairs={{0,160},{32,0},{128,32},{160,128},{1,161},{33,1},{129,33},{161,129... | collective-permute-start | bytes 983048 | tf_op jit(solution)/shard_map/ppermute | solution.py:233
  110.7 14.9 %collective-permute-start.8 = (bf16[1280,128]{1,0:T(8,128)(2,1)S(1)}, bf16[1280,128]{1,0:T(8,128)(2,1)S(1)}, u32[]{:S(2)}, u32[]{:S(2)}) collective-permute-start(bf16[1280,128]{1,0:T(8,128)(2,1)S(1)} %bitcast.18), channel_id=1, source_target_pairs={{0,128},{32,160},{128,0},{160,32},{1,129},{33,161},{129,1},{161,33... | collective-permute-start | bytes 983048 | tf_op jit(solution)/shard_map/ppermute | solution.py:233
  111.4 17.4 %collective-permute-start.7 = (bf16[1280,128]{1,0:T(8,128)(2,1)S(1)}, bf16[1280,128]{1,0:T(8,128)(2,1)S(1)}, u32[]{:S(2)}, u32[]{:S(2)}) collective-permute-start(bf16[1280,128]{1,0:T(8,128)(2,1)S(1)} %bitcast.19), channel_id=1, source_target_pairs={{0,32},{32,128},{128,160},{160,0},{1,33},{33,129},{129,161},{161,1... | collective-permute-start | bytes 983048 | tf_op jit(solution)/shard_map/ppermute | solution.py:233
  111.4 20.5 %collective-permute-start.10 = (bf16[1280,128]{1,0:T(8,128)(2,1)S(1)}, bf16[1280,128]{1,0:T(8,128)(2,1)S(1)}, u32[]{:S(2)}, u32[]{:S(2)}) collective-permute-start(bf16[1280,128]{1,0:T(8,128)(2,1)S(1)} %bitcast.20), channel_id=1, source_target_pairs={{0,64},{64,0},{1,65},{65,1},{2,66},{66,2},{3,67},{67,3},{4,68},{68... | collective-permute-start | bytes 983048 | tf_op jit(solution)/shard_map/ppermute | solution.py:228
  116.2 15.8 %collective-permute-start.13 = (bf16[1280,128]{1,0:T(8,128)(2,1)S(1)}, bf16[1280,128]{1,0:T(8,128)(2,1)S(1)}, u32[]{:S(2)}, u32[]{:S(2)}) collective-permute-start(bf16[1280,128]{1,0:T(8,128)(2,1)S(1)} %collective-permute-done.9.refs_3_), channel_id=1, source_target_pairs={{0,64},{64,0},{1,65},{65,1},{2,66},{66,2},{3,67},{67,3},{4,68},{68... | collective-permute-start | bytes 983048 | tf_op jit(solution)/shard_map/ppermute | solution.py:228
  125.6 6.3 %collective-permute-start.12 = (bf16[1280,128]{1,0:T(8,128)(2,1)S(1)}, bf16[1280,128]{1,0:T(8,128)(2,1)S(1)}, u32[]{:S(2)}, u32[]{:S(2)}) collective-permute-start(bf16[1280,128]{1,0:T(8,128)(2,1)S(1)} %collective-permute-done.8.refs_2_), channel_id=1, source_target_pairs={{0,64},{64,0},{1,65},{65,1},{2,66},{66,2},{3,67},{67,3},{4,68},{68... | collective-permute-start | bytes 983048 | tf_op jit(solution)/shard_map/ppermute | solution.py:228
  128.8 3.1 %collective-permute-start.11 = (bf16[1280,128]{1,0:T(8,128)(2,1)S(1)}, bf16[1280,128]{1,0:T(8,128)(2,1)S(1)}, u32[]{:S(2)}, u32[]{:S(2)}) collective-permute-start(bf16[1280,128]{1,0:T(8,128)(2,1)S(1)} %collective-permute-done.7.refs_1_), channel_id=1, source_target_pairs={{0,64},{64,0},{1,65},{65,1},{2,66},{66,2},{3,67},{67,3},{4,68},{68... | collective-permute-start | bytes 983048 | tf_op jit(solution)/shard_map/ppermute | solution.py:228
  129.4 2.6 %collective-permute-start.14 = (bf16[32,128]{1,0:T(8,128)(2,1)S(1)}, bf16[32,128]{1,0:T(8,128)(2,1)S(1)}, u32[]{:S(2)}, u32[]{:S(2)}) collective-permute-start(bf16[32,128]{1,0:T(8,128)(2,1)S(1)} %bitcast.22), channel_id=1, source_target_pairs={{0,32},{32,0},{1,33},{33,1},{2,34},{34,2},{3,35},{35,3},{4,36},{36... | collective-permute-start | bytes 24584 | tf_op jit(solution)/shard_map/ppermute | solution.py:228

commit v2 on v1

--- a/solution.py
+++ b/solution.py
@@ -159,9 +159,10 @@
 
         def block(g, x, h, gc_ref, half, taps_ref, gain, dist):
             gcs = [gc_ref[pl.ds(t0 + k * dist, CHUNK), :] for k in range(3)]
-            gh = sum(cols_dot(gcs[k], taps_ref[k * WIDE : (k + 1) * WIDE, :]) for k in range(3))
-            for k in range(3):
-                add(half, TAPS_AT + 1024 * k, rows_dot(h, gcs[k]))
+            side = jnp.concatenate(gcs, axis=1)
+            taps = jnp.concatenate([taps_ref[k * WIDE : (k + 1) * WIDE, :] for k in range(3)], axis=1)
+            gh = cols_dot(side, taps)
+            add(half, TAPS_AT, rows_dot(h, side))
             gn = jnp.where(h > 0, gh, 0.0)
             s = lax.rsqrt(mean(x * x) + EPS)
             normed = x * s
@@ -247,8 +248,9 @@
     summed = jnp.sum(got[:, :PART].astype(F32), axis=0).astype(BF)
     whole = jnp.broadcast_to(summed[None], (peers, PART, LANES))
     whole = lax.all_to_all(whole, rest, 0, 0, tiled=True).reshape(-1, LANES)
+    whole, there = lax.optimization_barrier((whole, swap(loss, "x_lo", 1)))
     mine = [whole] + [shift(whole, X, k) for k in range(1, 4)]
-    return mine, [swap(piece, "core", 1) for piece in mine], loss, swap(loss, "x_lo", 1)
+    return mine, [swap(piece, "core", 1) for piece in mine], loss, there
 
 
 def spread_kernel(*refs):

time: 135 us -> 134 us (level)
  blocking collectives: 53.6 us -> 38.7 us
  starting transfers between devices: 27.6 us -> 35.6 us
  waiting for transfers between devices: 21.7 us -> 27.4 us
    all_to_all x1 -> x0, blocking collectives: 15 us -> none  [reduce_all(): whole = lax.all_to_all(whole, rest, 0, 0, tiled=True).reshape(-1, LANES)]
    all_to_all x0 -> x1, waiting for transfers between devices: none -> 5.66 us  [reduce_all(): whole = lax.all_to_all(whole, rest, 0, 0, tiled=True).reshape(-1, LANES)]
    all_to_all x0 -> x1, starting transfers between devices: none -> 4.25 us  [reduce_all(): whole = lax.all_to_all(whole, rest, 0, 0, tiled=True).reshape(-1, LANES)]
    ppermute x9, starting transfers between devices: 15.5 us -> 19.3 us  [swap(): return lax.ppermute(array, axis, [(i, i ^ mask) for i in range(count)])]
  transfers between devices with their start and end apart: 15 -> 16, of which waited for: 7 -> 9; matrix products, arithmetic and copies ran while one was open for 1% -> 1% of each run, Pallas kernels for 0% -> 0%
where the time goes in v2:
time: 134 us
  blocking collectives  38.7 us (29%)
  starting transfers between devices  35.6 us (27%)
  Pallas kernels  28.1 us (21%)
  waiting for transfers between devices  27.4 us (20%)
  other arithmetic  2.35 us (2%)
    pallas_call x1, Pallas kernels, compute(): pl.pallas_call(functools.partial(kernel, peers, loss_scale), out_shape=[j...  25.5 us
    all_to_all x1, blocking collectives, local(): both = lax.all_to_all(both, ctx, 0, 0, tiled=True)  21.2 us
    ppermute x9, starting transfers between devices, swap(): return lax.ppermute(array, axis, [(i, i ^ mask) for i in range(count)])  19.3 us
    ppermute x6, waiting for transfers between devices, shift(): lax.ppermute(array, axis, [(i, (i + by) % count) for i in range(count)])  18 us
    all_to_all x1, blocking collectives, reduce_all(): got = lax.all_to_all(message, rest, 0, 0, tiled=True)  17.5 us
    ppermute x6, starting transfers between devices, shift(): lax.ppermute(array, axis, [(i, (i + by) % count) for i in range(count)])  12.1 us
    all_to_all x1, waiting for transfers between devices, reduce_all(): whole = lax.all_to_all(whole, rest, 0, 0, tiled=True).reshape(-1, LANES)  5.66 us
    all_to_all x1, starting transfers between devices, reduce_all(): whole = lax.all_to_all(whole, rest, 0, 0, tiled=True).reshape(-1, LANES)  4.25 us
  transfers between devices with their start and end apart: 16, of which 9 were waited for; matrix products, arithmetic and copies ran while one was open for 1% of the time, Pallas kernels for 0%

profile of v2, /device:TPU:33, one launch (start us, length us, event | category | flops | bytes accessed | tf_op | source)
XLA Modules:
  0.0 133.8 jit_solution(285785110278083489)
XLA Ops:
  0.6 0.7 pad_add_fusion
  1.4 21.2 %all_to_all.15.both_ref = s32[64,2,128]{2,1,0:T(2,128)} all-to-all(s32[64,2,128]{2,1,0:T(2,128)S(1)} %bitcast.27), channel_id=1, replica_groups=mesh['x_hi'=2,'core'=2,'x_lo'=2,'y'=4,'z'=8] {'x_lo','y','z'}, dimensions={0} | all-to-all | bytes 131072 | tf_op jit(solution)/shard_map/all_to_all | solution.py:323
  22.6 25.5 %shard_map.186 = (bf16[32,128]{1,0:T(8,128)(2,1)}, f32[1280,128]{1,0:T(8,128)}, f32[1280,128]{1,0:T(8,128)}, f32[1280,128]{1,0:T(8,128)}, f32[1280,128]{1,0:T(8,...) custom-call(s32[64,2,128]{2,1,0:T(2,128)} %all_to_all.15.both_ref, ...), custom_call_target="tpu_custom_call" | custom-call | tf_op jit(solution)/shard_map/pallas_call | solution.py:200
  48.0 0.0 copy-start.2
  48.1 2.0 %collective-permute-start.1 = (f32[1280,128]{1,0:T(8,128)}, f32[1280,128]{1,0:T(8,128)S(1)}, u32[]{:S(2)}, u32[]{:S(2)}) collective-permute-start(f32[1280,128]{1,0:T(8,128)} %get-tuple-element.34), channel_id=1, source_target_pairs={{0,64},{64,0},{1,65},{65,1},{2,66},{66,2},{3,67},{67,3},{4,68},{68... | collective-permute-start | bytes 1966088 | tf_op jit(solution)/shard_map/ppermute | solution.py:229
  50.0 0.3 collective-permute-start.3
  50.3 0.2 collective-permute-start
  50.5 0.3 collective-permute-start.5
  50.8 1.1 collective-permute-done.1
  52.0 0.0 copy-start.1
  52.0 1.2 add_convert_fusion.3
  53.2 0.7 collective-permute-start.2
  53.8 0.0 collective-permute-done.3
  53.8 0.0 copy-done.2
  53.8 0.0 copy-start
  53.9 0.1 add_convert_fusion.2
  53.9 2.5 %collective-permute-start.4 = (bf16[1280,128]{1,0:T(8,128)(2,1)S(1)}, bf16[1280,128]{1,0:T(8,128)(2,1)S(1)}, u32[]{:S(2)}, u32[]{:S(2)}) collective-permute-start(bf16[1280,128]{1,0:T(8,128)(2,1)S(1)} %add_convert_fusion.2), channel_id=1, source_target_pairs={{0,128},{32,160},{128,0},{160,32},{1,129},{33,161},{129,1},{161,33... | collective-permute-start | bytes 983048 | tf_op jit(solution)/shard_map/ppermute | solution.py:234
  56.5 0.0 collective-permute-done.5
  56.5 0.0 copy-done.1
  56.5 0.1 add_convert_fusion.1
  56.5 0.0 copy-start.3
  56.5 1.6 %collective-permute-start.6 = (bf16[1280,128]{1,0:T(8,128)(2,1)S(1)}, bf16[1280,128]{1,0:T(8,128)(2,1)S(1)}, u32[]{:S(2)}, u32[]{:S(2)}) collective-permute-start(bf16[1280,128]{1,0:T(8,128)(2,1)S(1)} %add_convert_fusion.1), channel_id=1, source_target_pairs={{0,160},{32,0},{128,32},{160,128},{1,161},{33,1},{129,33},{161,129... | collective-permute-start | bytes 983048 | tf_op jit(solution)/shard_map/ppermute | solution.py:234
  58.1 0.0 collective-permute-done
  58.1 5.3 %collective-permute-done.2 = bf16[1280,128]{1,0:T(8,128)(2,1)S(1)} collective-permute-done((bf16[1280,128]{1,0:T(8,128)(2,1)S(1)}, bf16[1280,128]{1,0:T(8,128)(2,1)S(1)}, u32[]{:S(2)}, u32[]{:S(2)}) %collective-permute-start.2) | collective-permute-done | bytes 327712 | tf_op jit(solution)/shard_map/ppermute | solution.py:234
  63.4 7.4 %collective-permute-done.4 = bf16[1280,128]{1,0:T(8,128)(2,1)S(1)} collective-permute-done((bf16[1280,128]{1,0:T(8,128)(2,1)S(1)}, bf16[1280,128]{1,0:T(8,128)(2,1)S(1)}, u32[]{:S(2)}, u32[]{:S(2)}) %collective-permute-start.4) | collective-permute-done | bytes 327712 | tf_op jit(solution)/shard_map/ppermute | solution.py:234
  70.8 0.1 collective-permute-done.6
  70.9 0.0 copy-done
  70.9 0.2 add_convert_fusion
  71.1 0.0 copy-done.3
  71.1 17.5 %all_to_all.16 = bf16[32,48,128]{2,1,0:T(8,128)(2,1)S(1)} all-to-all(bf16[32,48,128]{2,1,0:T(8,128)(2,1)S(1)} %pad_maximum_fusion), channel_id=1, replica_groups=mesh['x_hi'=2,'core'=2,'x_lo'=2,'y'=4,'z'=8] {'y','z'}, dimensions={0} | all-to-all | bytes 786432 | tf_op jit(solution)/shard_map/all_to_all | solution.py:246
  88.6 0.1 slice_reduce_fusion
  88.7 0.8 broadcast_in_dim.32
  89.4 4.2 %all-to-all-start.2 = ((bf16[32,40,128]{2,1,0:T(8,128)(2,1)}), bf16[32,40,128]{2,1,0:T(8,128)(2,1)S(1)}, u32[]{:S(2)}, u32[]{:S(2)}) async-start(bf16[32,40,128]{2,1,0:T(8,128)(2,1)} %broadcast_in_dim.32), calls=%async_computation.2 | async-start | bytes 655360 | tf_op jit(solution)/shard_map/all_to_all | solution.py:250
  93.7 3.9 %collective-permute-start.7 = (bf16[32,128]{1,0:T(8,128)(2,1)S(1)}, bf16[32,128]{1,0:T(8,128)(2,1)S(1)}, u32[]{:S(2)}, u32[]{:S(2)}) collective-permute-start(bf16[32,128]{1,0:T(8,128)(2,1)S(1)} %bitcast.22), channel_id=1, source_target_pairs={{0,32},{32,0},{1,33},{33,1},{2,34},{34,2},{3,35},{35,3},{4,36},{36... | collective-permute-start | bytes 24584 | tf_op jit(solution)/shard_map/ppermute | solution.py:229
  97.6 1.3 collective-permute-done.7.refs_9_
  99.0 5.7 %all-to-all-done.2 = bf16[32,40,128]{2,1,0:T(8,128)(2,1)S(1)} async-done(((bf16[32,40,128]{2,1,0:T(8,128)(2,1)}), bf16[32,40,128]{2,1,0:T(8,128)(2,1)S(1)}, u32[]{:S(2)}, u32[]{:S(2)}) %all-to-all-start.2) | async-done | bytes 327712 | tf_op jit(solution)/shard_map/all_to_all | solution.py:250
  104.6 6.6 %collective-permute-start.10 = (bf16[1280,128]{1,0:T(8,128)(2,1)S(1)}, bf16[1280,128]{1,0:T(8,128)(2,1)S(1)}, u32[]{:S(2)}, u32[]{:S(2)}) collective-permute-start(bf16[1280,128]{1,0:T(8,128)(2,1)S(1)} %bitcast.17), channel_id=1, source_target_pairs={{0,160},{32,0},{128,32},{160,128},{1,161},{33,1},{129,33},{161,129... | collective-permute-start | bytes 983048 | tf_op jit(solution)/shard_map/ppermute | solution.py:234
  111.2 0.7 collective-permute-start.9
  111.9 0.0 collective-permute-start.8
  111.9 2.7 %collective-permute-start.11 = (bf16[1280,128]{1,0:T(8,128)(2,1)S(1)}, bf16[1280,128]{1,0:T(8,128)(2,1)S(1)}, u32[]{:S(2)}, u32[]{:S(2)}) collective-permute-start(bf16[1280,128]{1,0:T(8,128)(2,1)S(1)} %bitcast.20), channel_id=1, source_target_pairs={{0,64},{64,0},{1,65},{65,1},{2,66},{66,2},{3,67},{67,3},{4,68},{68... | collective-permute-start | bytes 983048 | tf_op jit(solution)/shard_map/ppermute | solution.py:229
  114.7 2.1 %collective-permute-done.10.refs_3_ = bf16[1280,128]{1,0:T(8,128)(2,1)S(1)} collective-permute-done((bf16[1280,128]{1,0:T(8,128)(2,1)S(1)}, bf16[1280,128]{1,0:T(8,128)(2,1)S(1)}, u32[]{:S(2)}, u32[]{:S(2)}) %collective-permute-start.10) | collective-permute-done | bytes 327712 | tf_op jit(solution)/shard_map/ppermute | solution.py:234
  116.8 9.4 %collective-permute-start.14 = (bf16[1280,128]{1,0:T(8,128)(2,1)S(1)}, bf16[1280,128]{1,0:T(8,128)(2,1)S(1)}, u32[]{:S(2)}, u32[]{:S(2)}) collective-permute-start(bf16[1280,128]{1,0:T(8,128)(2,1)S(1)} %collective-permute-done.10.refs_3_), channel_id=1, source_target_pairs={{0,64},{64,0},{1,65},{65,1},{2,66},{66,2},{3,67},{67,3},{4,68},{68... | collective-permute-start | bytes 983048 | tf_op jit(solution)/shard_map/ppermute | solution.py:229
  126.2 0.0 collective-permute-done.9.refs_2_
  126.2 0.0 collective-permute-start.13
  126.2 3.2 %collective-permute-done.8.refs_1_ = bf16[1280,128]{1,0:T(8,128)(2,1)S(1)} collective-permute-done((bf16[1280,128]{1,0:T(8,128)(2,1)S(1)}, bf16[1280,128]{1,0:T(8,128)(2,1)S(1)}, u32[]{:S(2)}, u32[]{:S(2)}) %collective-permute-start.8) | collective-permute-done | bytes 327712 | tf_op jit(solution)/shard_map/ppermute | solution.py:234
  129.4 0.5 collective-permute-start.12
  129.9 0.0 collective-permute-done.11.refs_4_
  129.9 0.0 collective-permute-done.14.refs_7_
  129.9 0.0 collective-permute-done.13.refs_6_
  129.9 1.2 collective-permute-done.12.refs_5_
  131.1 2.6 %shard_map.187 = (f32[16,128]{1,0:T(8,128)}, f32[256,256]{1,0:T(8,128)}, f32[1,256]{1,0:T(1,128)}, f32[3,256,512]{2,1,0:T(8,128)}, f32[512,256]{1,0:T(8,128)}, /...) custom-call(bf16[1280,128]{1,0:T(8,128)(2,1)S(1)} %bitcast.21, ...), custom_call_target="tpu_custom_call" | custom-call | tf_op jit(solution)/shard_map/pallas_call | solution.py:306
  (6 shorter events, 0.1 us)
Async XLA Ops:
  48.0 5.8 %copy-start.2 = (f32[1280,128]{1,0:T(8,128)S(1)}, f32[1280,128]{1,0:T(8,128)}, u32[]{:S(2)}) copy-start(f32[1280,128]{1,0:T(8,128)} %get-tuple-element.35) | copy-start | bytes 1966084
  48.1 3.9 %collective-permute-start.1 = (f32[1280,128]{1,0:T(8,128)}, f32[1280,128]{1,0:T(8,128)S(1)}, u32[]{:S(2)}, u32[]{:S(2)}) collective-permute-start(f32[1280,128]{1,0:T(8,128)} %get-tuple-element.34), channel_id=1, source_target_pairs={{0,64},{64,0},{1,65},{65,1},{2,66},{66,2},{3,67},{67,3},{4,68},{68... | collective-permute-start | bytes 1966088 | tf_op jit(solution)/shard_map/ppermute | solution.py:229
  50.0 3.8 %collective-permute-start.3 = (f32[1280,128]{1,0:T(8,128)}, f32[1280,128]{1,0:T(8,128)S(1)}, u32[]{:S(2)}, u32[]{:S(2)}) collective-permute-start(f32[1280,128]{1,0:T(8,128)} %get-tuple-element.36), channel_id=1, source_target_pairs={{0,64},{64,0},{1,65},{65,1},{2,66},{66,2},{3,67},{67,3},{4,68},{68... | collective-permute-start | bytes 1966088 | tf_op jit(solution)/shard_map/ppermute | solution.py:229
  50.3 7.8 %collective-permute-start = (f32[1280,128]{1,0:T(8,128)}, f32[1280,128]{1,0:T(8,128)S(1)}, u32[]{:S(2)}, u32[]{:S(2)}) collective-permute-start(f32[1280,128]{1,0:T(8,128)} %get-tuple-element.32), channel_id=1, source_target_pairs={{0,64},{64,0},{1,65},{65,1},{2,66},{66,2},{3,67},{67,3},{4,68},{68... | collective-permute-start | bytes 1966088 | tf_op jit(solution)/shard_map/ppermute | solution.py:229
  50.5 5.9 %collective-permute-start.5 = (f32[1280,128]{1,0:T(8,128)}, f32[1280,128]{1,0:T(8,128)S(1)}, u32[]{:S(2)}, u32[]{:S(2)}) collective-permute-start(f32[1280,128]{1,0:T(8,128)} %get-tuple-element.38), channel_id=1, source_target_pairs={{0,64},{64,0},{1,65},{65,1},{2,66},{66,2},{3,67},{67,3},{4,68},{68... | collective-permute-start | bytes 1966088 | tf_op jit(solution)/shard_map/ppermute | solution.py:229
  52.0 4.5 %copy-start.1 = (f32[1280,128]{1,0:T(8,128)S(1)}, f32[1280,128]{1,0:T(8,128)}, u32[]{:S(2)}) copy-start(f32[1280,128]{1,0:T(8,128)} %get-tuple-element.37) | copy-start | bytes 1966084
  53.2 10.2 %collective-permute-start.2 = (bf16[1280,128]{1,0:T(8,128)(2,1)S(1)}, bf16[1280,128]{1,0:T(8,128)(2,1)S(1)}, u32[]{:S(2)}, u32[]{:S(2)}) collective-permute-start(bf16[1280,128]{1,0:T(8,128)(2,1)S(1)} %add_convert_fusion.3), channel_id=1, source_target_pairs={{0,32},{32,128},{128,160},{160,0},{1,33},{33,129},{129,161},{161,1... | collective-permute-start | bytes 983048 | tf_op jit(solution)/shard_map/ppermute | solution.py:234
  53.8 17.0 %copy-start = (f32[1280,128]{1,0:T(8,128)S(1)}, f32[1280,128]{1,0:T(8,128)}, u32[]{:S(2)}) copy-start(f32[1280,128]{1,0:T(8,128)} %get-tuple-element.31) | copy-start | bytes 1966084
  53.9 16.8 %collective-permute-start.4 = (bf16[1280,128]{1,0:T(8,128)(2,1)S(1)}, bf16[1280,128]{1,0:T(8,128)(2,1)S(1)}, u32[]{:S(2)}, u32[]{:S(2)}) collective-permute-start(bf16[1280,128]{1,0:T(8,128)(2,1)S(1)} %add_convert_fusion.2), channel_id=1, source_target_pairs={{0,128},{32,160},{128,0},{160,32},{1,129},{33,161},{129,1},{161,33... | collective-permute-start | bytes 983048 | tf_op jit(solution)/shard_map/ppermute | solution.py:234
  56.5 14.5 %copy-start.3 = (bf16[32,128]{1,0:T(8,128)(2,1)S(1)}, bf16[32,128]{1,0:T(8,128)(2,1)}, u32[]{:S(2)}) copy-start(bf16[32,128]{1,0:T(8,128)(2,1)} %get-tuple-element.39) | copy-start | bytes 24580
  56.5 14.3 %collective-permute-start.6 = (bf16[1280,128]{1,0:T(8,128)(2,1)S(1)}, bf16[1280,128]{1,0:T(8,128)(2,1)S(1)}, u32[]{:S(2)}, u32[]{:S(2)}) collective-permute-start(bf16[1280,128]{1,0:T(8,128)(2,1)S(1)} %add_convert_fusion.1), channel_id=1, source_target_pairs={{0,160},{32,0},{128,32},{160,128},{1,161},{33,1},{129,33},{161,129... | collective-permute-start | bytes 983048 | tf_op jit(solution)/shard_map/ppermute | solution.py:234
  89.4 15.2 %all-to-all-start.2 = ((bf16[32,40,128]{2,1,0:T(8,128)(2,1)}), bf16[32,40,128]{2,1,0:T(8,128)(2,1)S(1)}, u32[]{:S(2)}, u32[]{:S(2)}) async-start(bf16[32,40,128]{2,1,0:T(8,128)(2,1)} %broadcast_in_dim.32), calls=%async_computation.2 | async-start | bytes 655360 | tf_op jit(solution)/shard_map/all_to_all | solution.py:250
  93.7 5.2 %collective-permute-start.7 = (bf16[32,128]{1,0:T(8,128)(2,1)S(1)}, bf16[32,128]{1,0:T(8,128)(2,1)S(1)}, u32[]{:S(2)}, u32[]{:S(2)}) collective-permute-start(bf16[32,128]{1,0:T(8,128)(2,1)S(1)} %bitcast.22), channel_id=1, source_target_pairs={{0,32},{32,0},{1,33},{33,1},{2,34},{34,2},{3,35},{35,3},{4,36},{36... | collective-permute-start | bytes 24584 | tf_op jit(solution)/shard_map/ppermute | solution.py:229
  104.6 12.1 %collective-permute-start.10 = (bf16[1280,128]{1,0:T(8,128)(2,1)S(1)}, bf16[1280,128]{1,0:T(8,128)(2,1)S(1)}, u32[]{:S(2)}, u32[]{:S(2)}) collective-permute-start(bf16[1280,128]{1,0:T(8,128)(2,1)S(1)} %bitcast.17), channel_id=1, source_target_pairs={{0,160},{32,0},{128,32},{160,128},{1,161},{33,1},{129,33},{161,129... | collective-permute-start | bytes 983048 | tf_op jit(solution)/shard_map/ppermute | solution.py:234
  111.2 14.9 %collective-permute-start.9 = (bf16[1280,128]{1,0:T(8,128)(2,1)S(1)}, bf16[1280,128]{1,0:T(8,128)(2,1)S(1)}, u32[]{:S(2)}, u32[]{:S(2)}) collective-permute-start(bf16[1280,128]{1,0:T(8,128)(2,1)S(1)} %bitcast.18), channel_id=1, source_target_pairs={{0,128},{32,160},{128,0},{160,32},{1,129},{33,161},{129,1},{161,33... | collective-permute-start | bytes 983048 | tf_op jit(solution)/shard_map/ppermute | solution.py:234
  111.9 17.4 %collective-permute-start.8 = (bf16[1280,128]{1,0:T(8,128)(2,1)S(1)}, bf16[1280,128]{1,0:T(8,128)(2,1)S(1)}, u32[]{:S(2)}, u32[]{:S(2)}) collective-permute-start(bf16[1280,128]{1,0:T(8,128)(2,1)S(1)} %bitcast.19), channel_id=1, source_target_pairs={{0,32},{32,128},{128,160},{160,0},{1,33},{33,129},{129,161},{161,1... | collective-permute-start | bytes 983048 | tf_op jit(solution)/shard_map/ppermute | solution.py:234
  111.9 17.9 %collective-permute-start.11 = (bf16[1280,128]{1,0:T(8,128)(2,1)S(1)}, bf16[1280,128]{1,0:T(8,128)(2,1)S(1)}, u32[]{:S(2)}, u32[]{:S(2)}) collective-permute-start(bf16[1280,128]{1,0:T(8,128)(2,1)S(1)} %bitcast.20), channel_id=1, source_target_pairs={{0,64},{64,0},{1,65},{65,1},{2,66},{66,2},{3,67},{67,3},{4,68},{68... | collective-permute-start | bytes 983048 | tf_op jit(solution)/shard_map/ppermute | solution.py:229
  116.8 13.1 %collective-permute-start.14 = (bf16[1280,128]{1,0:T(8,128)(2,1)S(1)}, bf16[1280,128]{1,0:T(8,128)(2,1)S(1)}, u32[]{:S(2)}, u32[]{:S(2)}) collective-permute-start(bf16[1280,128]{1,0:T(8,128)(2,1)S(1)} %collective-permute-done.10.refs_3_), channel_id=1, source_target_pairs={{0,64},{64,0},{1,65},{65,1},{2,66},{66,2},{3,67},{67,3},{4,68},{68... | collective-permute-start | bytes 983048 | tf_op jit(solution)/shard_map/ppermute | solution.py:229
  126.2 3.7 %collective-permute-start.13 = (bf16[1280,128]{1,0:T(8,128)(2,1)S(1)}, bf16[1280,128]{1,0:T(8,128)(2,1)S(1)}, u32[]{:S(2)}, u32[]{:S(2)}) collective-permute-start(bf16[1280,128]{1,0:T(8,128)(2,1)S(1)} %collective-permute-done.9.refs_2_), channel_id=1, source_target_pairs={{0,64},{64,0},{1,65},{65,1},{2,66},{66,2},{3,67},{67,3},{4,68},{68... | collective-permute-start | bytes 983048 | tf_op jit(solution)/shard_map/ppermute | solution.py:229
  129.4 1.8 %collective-permute-start.12 = (bf16[1280,128]{1,0:T(8,128)(2,1)S(1)}, bf16[1280,128]{1,0:T(8,128)(2,1)S(1)}, u32[]{:S(2)}, u32[]{:S(2)}) collective-permute-start(bf16[1280,128]{1,0:T(8,128)(2,1)S(1)} %collective-permute-done.8.refs_1_), channel_id=1, source_target_pairs={{0,64},{64,0},{1,65},{65,1},{2,66},{66,2},{3,67},{67,3},{4,68},{68... | collective-permute-start | bytes 983048 | tf_op jit(solution)/shard_map/ppermute | solution.py:229

commit v3 on v2

--- a/solution.py
+++ b/solution.py
@@ -24,12 +24,21 @@
     return lax.dot_general(left, right, (((0,), (0,)), ((), ())), preferred_element_type=F32)
 
 
+def by_halves(product, left, right, wide):
+    if wide > WIDE:
+        return product(left, right)
+    half = left.shape[0] // 2
+    return jnp.concatenate([product(left[:half], right), product(left[half:], right)], axis=0)
+
+
 def cols_dot(left, right):
-    return lax.dot_general(left, right, (((1,), (1,)), ((), ())), preferred_element_type=F32)
+    product = lambda a, b: lax.dot_general(a, b, (((1,), (1,)), ((), ())), preferred_element_type=F32)
+    return by_halves(product, left, right, right.shape[0])
 
 
 def dot(left, right):
-    return jnp.dot(left, right, preferred_element_type=F32)
+    product = lambda a, b: jnp.dot(a, b, preferred_element_type=F32)
+    return by_halves(product, left, right, right.shape[1])
 
 
 def mean(values):
@@ -56,7 +65,8 @@
     keep_refs, send_refs = rest[:4], rest[4:8]
     (embed_ref, gain1_ref, taps1_ref, out1_ref, gain2_ref, taps2_ref, out2_ref, gainf_ref, head_ref) = rest[8:17]
     (sems, tok_ref, targ_ref, hot_ref, x0_ref, h1_ref, a1_ref, x1_ref, h2_ref, a2_ref, gx2_ref, gc2_ref, gc1_ref) = rest[17:30]
-    losses_ref, acc_ref = rest[30:]
+    losses_ref, acc0_ref, acc1_ref, out_sems = rest[30:]
+    accs = (acc0_ref, acc1_ref)
     sources = (embed_hbm, gain1_hbm, taps1_hbm, out1_hbm, gain2_hbm, taps2_hbm, out2_hbm, gainf_hbm, head_hbm)
     copies = [pltpu.make_async_copy(src, dst, sems.at[i]) for i, (src, dst) in enumerate(zip(sources, rest[8:17]))]
     for copy in copies:
@@ -69,7 +79,8 @@
     h2_ref[0:LEAD, :] = zeros
     gc1_ref[rows : rows + LEAD, :] = jnp.zeros((LEAD, 2 * WIDE), BF)
     gc2_ref[rows : rows + LEAD, :] = jnp.zeros((LEAD, 2 * WIDE), BF)
-    acc_ref[...] = jnp.zeros_like(acc_ref)
+    acc0_ref[...] = jnp.zeros_like(acc0_ref)
+    acc1_ref[...] = jnp.zeros_like(acc1_ref)
     quarter = lax.rem(lax.axis_index("z"), 4)
 
     def mine(block):
@@ -94,7 +105,7 @@
         height = value.shape[0]
         for b in range(value.shape[1] // LANES):
             start = at + b * height
-            acc_ref[half, start : start + height, :] += value[:, b * LANES : (b + 1) * LANES]
+            accs[half][start : start + height, :] += value[:, b * LANES : (b + 1) * LANES]
 
     for copy in copies:
         copy.wait()
@@ -152,6 +163,22 @@
     half = peers
     loss_ref[...] = jnp.concatenate([high[:half], low[:half], high[half:], low[half:]], axis=1).astype(BF)
 
+    core, x = lax.axis_index("core"), lax.axis_index(X)
+
+    def leave(half, begin):
+        for kept in (True, False):
+            targets = keep_refs if kept else send_refs
+
+            @pl.when((core == half) == kept)
+            def _():
+                for k in range(4):
+                    at = pl.ds(pl.multiple_of(lax.rem(x + k, 4) * part, part), part)
+                    copy = pltpu.make_async_copy(accs[half].at[at, :], targets[k], out_sems.at[half, k])
+                    if begin:
+                        copy.start()
+                    else:
+                        copy.wait()
+
     def back(i, carry):
         j = n - 1 - i
         t0 = pl.multiple_of(j * CHUNK, CHUNK)
@@ -172,6 +199,11 @@
 
         h2 = h2_ref[pl.ds(t0 + LEAD, CHUNK), :]
         gx1 = block(gx2_ref[here, :], x1_ref[here, :], h2, gc2_ref, 1, taps2_ref, gain2_ref[...], 2 * STEP)
+
+        @pl.when(i == n - 1)
+        def _():
+            leave(1, True)
+
         low = gx1.astype(BF)
         a = a1_ref[here, :]
         add(0, OUT_AT, rows_dot(a, low))
@@ -184,11 +216,9 @@
 
     lax.fori_loop(0, n, back, 0)
 
-    core, x = lax.axis_index("core"), lax.axis_index(X)
-    for k in range(4):
-        at = pl.ds(pl.multiple_of(lax.rem(x + k, 4) * part, part), part)
-        keep_refs[k][...] = acc_ref[core, at, :]
-        send_refs[k][...] = acc_ref[1 - core, at, :]
+    leave(0, True)
+    leave(1, False)
+    leave(0, False)
 
 
 def compute(both, weights, loss_scale, peers):
@@ -201,7 +231,7 @@
         functools.partial(kernel, peers, loss_scale),
         out_shape=[jax.ShapeDtypeStruct((peers, LANES), BF)] + [jax.ShapeDtypeStruct((part, LANES), F32)] * 8,
         in_specs=[vmem] + [hbm] * len(weights),
-        out_specs=[vmem] * 9,
+        out_specs=[vmem] + [hbm] * 8,
         scratch_shapes=[pltpu.VMEM(w.shape, w.dtype) for w in weights]
         + [
             pltpu.SemaphoreType.DMA((len(weights),)),
@@ -218,7 +248,9 @@
             tall(2 * WIDE, BF, LEAD),
             tall(2 * WIDE, BF, LEAD),
             pltpu.VMEM((rows // STEP, STEP), F32),
-            pltpu.VMEM((2, 4 * part, LANES), F32),
+            pltpu.VMEM((4 * part, LANES), F32),
+            pltpu.VMEM((4 * part, LANES), F32),
+            pltpu.SemaphoreType.DMA((2, 4)),
         ],
         compiler_params=pltpu.CompilerParams(vmem_limit_bytes=57 * 2**20),
     )(both, *weights)

time: 134 us -> 134 us (level)
  no operation moved by 1% of the time
where the time goes in v3:
time: 134 us; the launch traced here: 133 us
  blocking collectives  38.7 us (29%)
  starting transfers between devices  35.9 us (27%)
  waiting for transfers between devices  27.6 us (21%)
  Pallas kernels  27 us (20%)
  other arithmetic  2.35 us (2%)
    pallas_call x1, Pallas kernels, compute(): pl.pallas_call(functools.partial(kernel, peers, loss_scale), out_shape=[j...  24.4 us
    all_to_all x1, blocking collectives, local(): both = lax.all_to_all(both, ctx, 0, 0, tiled=True)  21.2 us
    ppermute x9, starting transfers between devices, swap(): return lax.ppermute(array, axis, [(i, i ^ mask) for i in range(count)])  19.6 us
    ppermute x6, waiting for transfers between devices, shift(): lax.ppermute(array, axis, [(i, (i + by) % count) for i in range(count)])  18 us
    all_to_all x1, blocking collectives, reduce_all(): got = lax.all_to_all(message, rest, 0, 0, tiled=True)  17.5 us
    ppermute x6, starting transfers between devices, shift(): lax.ppermute(array, axis, [(i, (i + by) % count) for i in range(count)])  12.1 us
    all_to_all x1, waiting for transfers between devices, reduce_all(): whole = lax.all_to_all(whole, rest, 0, 0, tiled=True).reshape(-1, LANES)  5.66 us
    all_to_all x1, starting transfers between devices, reduce_all(): whole = lax.all_to_all(whole, rest, 0, 0, tiled=True).reshape(-1, LANES)  4.25 us
  transfers between devices with their start and end apart: 16, of which 9 were waited for; matrix products, arithmetic and copies ran while one was open for 1% of the time, Pallas kernels for 0%

profile of v3, /device:TPU:33, one launch (start us, length us, event | category | flops | bytes accessed | tf_op | source)
XLA Modules:
  0.0 133.2 jit_solution(10696606758827979563)
XLA Ops:
  0.6 0.7 pad_add_fusion
  1.4 21.2 %all_to_all.15.both_ref = s32[64,2,128]{2,1,0:T(2,128)} all-to-all(s32[64,2,128]{2,1,0:T(2,128)S(1)} %bitcast.27), channel_id=1, replica_groups=mesh['x_hi'=2,'core'=2,'x_lo'=2,'y'=4,'z'=8] {'x_lo','y','z'}, dimensions={0} | all-to-all | bytes 131072 | tf_op jit(solution)/shard_map/all_to_all | solution.py:355
  22.6 24.4 %shard_map.186 = (bf16[32,128]{1,0:T(8,128)(2,1)}, f32[1280,128]{1,0:T(8,128)}, f32[1280,128]{1,0:T(8,128)}, f32[1280,128]{1,0:T(8,128)}, f32[1280,128]{1,0:T(8,...) custom-call(s32[64,2,128]{2,1,0:T(2,128)} %all_to_all.15.both_ref, ...), custom_call_target="tpu_custom_call" | custom-call | tf_op jit(solution)/shard_map/pallas_call | solution.py:230
  47.0 0.0 copy-start.2
  47.0 2.4 %collective-permute-start.1 = (f32[1280,128]{1,0:T(8,128)}, f32[1280,128]{1,0:T(8,128)S(1)}, u32[]{:S(2)}, u32[]{:S(2)}) collective-permute-start(f32[1280,128]{1,0:T(8,128)} %get-tuple-element.34), channel_id=1, source_target_pairs={{0,64},{64,0},{1,65},{65,1},{2,66},{66,2},{3,67},{67,3},{4,68},{68... | collective-permute-start | bytes 1966088 | tf_op jit(solution)/shard_map/ppermute | solution.py:261
  49.4 0.1 collective-permute-start.3
  49.5 0.4 collective-permute-start
  49.9 0.1 collective-permute-start.5
  50.0 1.3 collective-permute-done.1
  51.4 0.0 copy-start.1
  51.4 1.2 add_convert_fusion.3
  52.6 0.7 collective-permute-start.2
  53.3 0.0 collective-permute-done.3
  53.3 0.0 copy-done.2
  53.3 0.0 copy-start
  53.3 0.1 add_convert_fusion.2
  53.3 2.5 %collective-permute-start.4 = (bf16[1280,128]{1,0:T(8,128)(2,1)S(1)}, bf16[1280,128]{1,0:T(8,128)(2,1)S(1)}, u32[]{:S(2)}, u32[]{:S(2)}) collective-permute-start(bf16[1280,128]{1,0:T(8,128)(2,1)S(1)} %add_convert_fusion.2), channel_id=1, source_target_pairs={{0,128},{32,160},{128,0},{160,32},{1,129},{33,161},{129,1},{161,33... | collective-permute-start | bytes 983048 | tf_op jit(solution)/shard_map/ppermute | solution.py:266
  55.9 0.0 collective-permute-done.5
  55.9 0.0 copy-done.1
  55.9 0.1 add_convert_fusion.1
  55.9 0.0 copy-start.3
  56.0 1.6 %collective-permute-start.6 = (bf16[1280,128]{1,0:T(8,128)(2,1)S(1)}, bf16[1280,128]{1,0:T(8,128)(2,1)S(1)}, u32[]{:S(2)}, u32[]{:S(2)}) collective-permute-start(bf16[1280,128]{1,0:T(8,128)(2,1)S(1)} %add_convert_fusion.1), channel_id=1, source_target_pairs={{0,160},{32,0},{128,32},{160,128},{1,161},{33,1},{129,33},{161,129... | collective-permute-start | bytes 983048 | tf_op jit(solution)/shard_map/ppermute | solution.py:266
  57.5 0.0 collective-permute-done
  57.5 5.3 %collective-permute-done.2 = bf16[1280,128]{1,0:T(8,128)(2,1)S(1)} collective-permute-done((bf16[1280,128]{1,0:T(8,128)(2,1)S(1)}, bf16[1280,128]{1,0:T(8,128)(2,1)S(1)}, u32[]{:S(2)}, u32[]{:S(2)}) %collective-permute-start.2) | collective-permute-done | bytes 327712 | tf_op jit(solution)/shard_map/ppermute | solution.py:266
  62.8 7.4 %collective-permute-done.4 = bf16[1280,128]{1,0:T(8,128)(2,1)S(1)} collective-permute-done((bf16[1280,128]{1,0:T(8,128)(2,1)S(1)}, bf16[1280,128]{1,0:T(8,128)(2,1)S(1)}, u32[]{:S(2)}, u32[]{:S(2)}) %collective-permute-start.4) | collective-permute-done | bytes 327712 | tf_op jit(solution)/shard_map/ppermute | solution.py:266
  70.2 0.1 collective-permute-done.6
  70.3 0.0 copy-done
  70.3 0.2 add_convert_fusion
  70.5 0.0 copy-done.3
  70.5 17.5 %all_to_all.16 = bf16[32,48,128]{2,1,0:T(8,128)(2,1)S(1)} all-to-all(bf16[32,48,128]{2,1,0:T(8,128)(2,1)S(1)} %pad_maximum_fusion), channel_id=1, replica_groups=mesh['x_hi'=2,'core'=2,'x_lo'=2,'y'=4,'z'=8] {'y','z'}, dimensions={0} | all-to-all | bytes 786432 | tf_op jit(solution)/shard_map/all_to_all | solution.py:278
  88.0 0.1 slice_reduce_fusion
  88.1 0.8 broadcast_in_dim.32
  88.8 4.3 %all-to-all-start.2 = ((bf16[32,40,128]{2,1,0:T(8,128)(2,1)}), bf16[32,40,128]{2,1,0:T(8,128)(2,1)S(1)}, u32[]{:S(2)}, u32[]{:S(2)}) async-start(bf16[32,40,128]{2,1,0:T(8,128)(2,1)} %broadcast_in_dim.32), calls=%async_computation.2 | async-start | bytes 655360 | tf_op jit(solution)/shard_map/all_to_all | solution.py:282
  93.1 3.9 %collective-permute-start.7 = (bf16[32,128]{1,0:T(8,128)(2,1)S(1)}, bf16[32,128]{1,0:T(8,128)(2,1)S(1)}, u32[]{:S(2)}, u32[]{:S(2)}) collective-permute-start(bf16[32,128]{1,0:T(8,128)(2,1)S(1)} %bitcast.22), channel_id=1, source_target_pairs={{0,32},{32,0},{1,33},{33,1},{2,34},{34,2},{3,35},{35,3},{4,36},{36... | collective-permute-start | bytes 24584 | tf_op jit(solution)/shard_map/ppermute | solution.py:261
  97.0 1.3 %collective-permute-done.7.refs_9_ = bf16[32,128]{1,0:T(8,128)(2,1)S(1)} collective-permute-done((bf16[32,128]{1,0:T(8,128)(2,1)S(1)}, bf16[32,128]{1,0:T(8,128)(2,1)S(1)}, u32[]{:S(2)}, u32[]{:S(2)}) %collective-permute-start.7) | collective-permute-done | bytes 8224 | tf_op jit(solution)/shard_map/ppermute | solution.py:261
  98.4 5.7 %all-to-all-done.2 = bf16[32,40,128]{2,1,0:T(8,128)(2,1)S(1)} async-done(((bf16[32,40,128]{2,1,0:T(8,128)(2,1)}), bf16[32,40,128]{2,1,0:T(8,128)(2,1)S(1)}, u32[]{:S(2)}, u32[]{:S(2)}) %all-to-all-start.2) | async-done | bytes 327712 | tf_op jit(solution)/shard_map/all_to_all | solution.py:282
  104.0 6.6 %collective-permute-start.10 = (bf16[1280,128]{1,0:T(8,128)(2,1)S(1)}, bf16[1280,128]{1,0:T(8,128)(2,1)S(1)}, u32[]{:S(2)}, u32[]{:S(2)}) collective-permute-start(bf16[1280,128]{1,0:T(8,128)(2,1)S(1)} %bitcast.17), channel_id=1, source_target_pairs={{0,160},{32,0},{128,32},{160,128},{1,161},{33,1},{129,33},{161,129... | collective-permute-start | bytes 983048 | tf_op jit(solution)/shard_map/ppermute | solution.py:266
  110.6 0.7 collective-permute-start.9
  111.4 0.0 collective-permute-start.8
  111.4 2.7 %collective-permute-start.11 = (bf16[1280,128]{1,0:T(8,128)(2,1)S(1)}, bf16[1280,128]{1,0:T(8,128)(2,1)S(1)}, u32[]{:S(2)}, u32[]{:S(2)}) collective-permute-start(bf16[1280,128]{1,0:T(8,128)(2,1)S(1)} %bitcast.20), channel_id=1, source_target_pairs={{0,64},{64,0},{1,65},{65,1},{2,66},{66,2},{3,67},{67,3},{4,68},{68... | collective-permute-start | bytes 983048 | tf_op jit(solution)/shard_map/ppermute | solution.py:261
  114.1 2.1 %collective-permute-done.10.refs_3_ = bf16[1280,128]{1,0:T(8,128)(2,1)S(1)} collective-permute-done((bf16[1280,128]{1,0:T(8,128)(2,1)S(1)}, bf16[1280,128]{1,0:T(8,128)(2,1)S(1)}, u32[]{:S(2)}, u32[]{:S(2)}) %collective-permute-start.10) | collective-permute-done | bytes 327712 | tf_op jit(solution)/shard_map/ppermute | solution.py:266
  116.2 9.4 %collective-permute-start.14 = (bf16[1280,128]{1,0:T(8,128)(2,1)S(1)}, bf16[1280,128]{1,0:T(8,128)(2,1)S(1)}, u32[]{:S(2)}, u32[]{:S(2)}) collective-permute-start(bf16[1280,128]{1,0:T(8,128)(2,1)S(1)} %collective-permute-done.10.refs_3_), channel_id=1, source_target_pairs={{0,64},{64,0},{1,65},{65,1},{2,66},{66,2},{3,67},{67,3},{4,68},{68... | collective-permute-start | bytes 983048 | tf_op jit(solution)/shard_map/ppermute | solution.py:261
  125.6 0.0 collective-permute-done.9.refs_2_
  125.6 0.0 collective-permute-start.13
  125.6 3.2 %collective-permute-done.8.refs_1_ = bf16[1280,128]{1,0:T(8,128)(2,1)S(1)} collective-permute-done((bf16[1280,128]{1,0:T(8,128)(2,1)S(1)}, bf16[1280,128]{1,0:T(8,128)(2,1)S(1)}, u32[]{:S(2)}, u32[]{:S(2)}) %collective-permute-start.8) | collective-permute-done | bytes 327712 | tf_op jit(solution)/shard_map/ppermute | solution.py:266
  128.8 0.5 collective-permute-start.12
  129.3 0.0 collective-permute-done.11.refs_4_
  129.3 0.0 collective-permute-done.14.refs_7_
  129.3 0.0 collective-permute-done.13.refs_6_
  129.3 1.2 collective-permute-done.12.refs_5_
  130.6 2.6 %shard_map.187 = (f32[16,128]{1,0:T(8,128)}, f32[256,256]{1,0:T(8,128)}, f32[1,256]{1,0:T(1,128)}, f32[3,256,512]{2,1,0:T(8,128)}, f32[512,256]{1,0:T(8,128)}, /...) custom-call(bf16[1280,128]{1,0:T(8,128)(2,1)S(1)} %bitcast.21, ...), custom_call_target="tpu_custom_call" | custom-call | tf_op jit(solution)/shard_map/pallas_call | solution.py:338
  (6 shorter events, 0.1 us)
Async XLA Ops:
  47.0 6.3 %copy-start.2 = (f32[1280,128]{1,0:T(8,128)S(1)}, f32[1280,128]{1,0:T(8,128)}, u32[]{:S(2)}) copy-start(f32[1280,128]{1,0:T(8,128)} %get-tuple-element.35) | copy-start | bytes 1966084
  47.0 4.3 %collective-permute-start.1 = (f32[1280,128]{1,0:T(8,128)}, f32[1280,128]{1,0:T(8,128)S(1)}, u32[]{:S(2)}, u32[]{:S(2)}) collective-permute-start(f32[1280,128]{1,0:T(8,128)} %get-tuple-element.34), channel_id=1, source_target_pairs={{0,64},{64,0},{1,65},{65,1},{2,66},{66,2},{3,67},{67,3},{4,68},{68... | collective-permute-start | bytes 1966088 | tf_op jit(solution)/shard_map/ppermute | solution.py:261
  49.4 3.8 %collective-permute-start.3 = (f32[1280,128]{1,0:T(8,128)}, f32[1280,128]{1,0:T(8,128)S(1)}, u32[]{:S(2)}, u32[]{:S(2)}) collective-permute-start(f32[1280,128]{1,0:T(8,128)} %get-tuple-element.36), channel_id=1, source_target_pairs={{0,64},{64,0},{1,65},{65,1},{2,66},{66,2},{3,67},{67,3},{4,68},{68... | collective-permute-start | bytes 1966088 | tf_op jit(solution)/shard_map/ppermute | solution.py:261
  49.5 8.0 %collective-permute-start = (f32[1280,128]{1,0:T(8,128)}, f32[1280,128]{1,0:T(8,128)S(1)}, u32[]{:S(2)}, u32[]{:S(2)}) collective-permute-start(f32[1280,128]{1,0:T(8,128)} %get-tuple-element.32), channel_id=1, source_target_pairs={{0,64},{64,0},{1,65},{65,1},{2,66},{66,2},{3,67},{67,3},{4,68},{68... | collective-permute-start | bytes 1966088 | tf_op jit(solution)/shard_map/ppermute | solution.py:261
  49.9 5.9 %collective-permute-start.5 = (f32[1280,128]{1,0:T(8,128)}, f32[1280,128]{1,0:T(8,128)S(1)}, u32[]{:S(2)}, u32[]{:S(2)}) collective-permute-start(f32[1280,128]{1,0:T(8,128)} %get-tuple-element.38), channel_id=1, source_target_pairs={{0,64},{64,0},{1,65},{65,1},{2,66},{66,2},{3,67},{67,3},{4,68},{68... | collective-permute-start | bytes 1966088 | tf_op jit(solution)/shard_map/ppermute | solution.py:261
  51.4 4.5 %copy-start.1 = (f32[1280,128]{1,0:T(8,128)S(1)}, f32[1280,128]{1,0:T(8,128)}, u32[]{:S(2)}) copy-start(f32[1280,128]{1,0:T(8,128)} %get-tuple-element.37) | copy-start | bytes 1966084
  52.6 10.2 %collective-permute-start.2 = (bf16[1280,128]{1,0:T(8,128)(2,1)S(1)}, bf16[1280,128]{1,0:T(8,128)(2,1)S(1)}, u32[]{:S(2)}, u32[]{:S(2)}) collective-permute-start(bf16[1280,128]{1,0:T(8,128)(2,1)S(1)} %add_convert_fusion.3), channel_id=1, source_target_pairs={{0,32},{32,128},{128,160},{160,0},{1,33},{33,129},{129,161},{161,1... | collective-permute-start | bytes 983048 | tf_op jit(solution)/shard_map/ppermute | solution.py:266
  53.3 17.0 %copy-start = (f32[1280,128]{1,0:T(8,128)S(1)}, f32[1280,128]{1,0:T(8,128)}, u32[]{:S(2)}) copy-start(f32[1280,128]{1,0:T(8,128)} %get-tuple-element.31) | copy-start | bytes 1966084
  53.3 16.8 %collective-permute-start.4 = (bf16[1280,128]{1,0:T(8,128)(2,1)S(1)}, bf16[1280,128]{1,0:T(8,128)(2,1)S(1)}, u32[]{:S(2)}, u32[]{:S(2)}) collective-permute-start(bf16[1280,128]{1,0:T(8,128)(2,1)S(1)} %add_convert_fusion.2), channel_id=1, source_target_pairs={{0,128},{32,160},{128,0},{160,32},{1,129},{33,161},{129,1},{161,33... | collective-permute-start | bytes 983048 | tf_op jit(solution)/shard_map/ppermute | solution.py:266
  55.9 14.5 %copy-start.3 = (bf16[32,128]{1,0:T(8,128)(2,1)S(1)}, bf16[32,128]{1,0:T(8,128)(2,1)}, u32[]{:S(2)}) copy-start(bf16[32,128]{1,0:T(8,128)(2,1)} %get-tuple-element.39) | copy-start | bytes 24580
  56.0 14.3 %collective-permute-start.6 = (bf16[1280,128]{1,0:T(8,128)(2,1)S(1)}, bf16[1280,128]{1,0:T(8,128)(2,1)S(1)}, u32[]{:S(2)}, u32[]{:S(2)}) collective-permute-start(bf16[1280,128]{1,0:T(8,128)(2,1)S(1)} %add_convert_fusion.1), channel_id=1, source_target_pairs={{0,160},{32,0},{128,32},{160,128},{1,161},{33,1},{129,33},{161,129... | collective-permute-start | bytes 983048 | tf_op jit(solution)/shard_map/ppermute | solution.py:266
  88.8 15.2 %all-to-all-start.2 = ((bf16[32,40,128]{2,1,0:T(8,128)(2,1)}), bf16[32,40,128]{2,1,0:T(8,128)(2,1)S(1)}, u32[]{:S(2)}, u32[]{:S(2)}) async-start(bf16[32,40,128]{2,1,0:T(8,128)(2,1)} %broadcast_in_dim.32), calls=%async_computation.2 | async-start | bytes 655360 | tf_op jit(solution)/shard_map/all_to_all | solution.py:282
  93.1 5.2 %collective-permute-start.7 = (bf16[32,128]{1,0:T(8,128)(2,1)S(1)}, bf16[32,128]{1,0:T(8,128)(2,1)S(1)}, u32[]{:S(2)}, u32[]{:S(2)}) collective-permute-start(bf16[32,128]{1,0:T(8,128)(2,1)S(1)} %bitcast.22), channel_id=1, source_target_pairs={{0,32},{32,0},{1,33},{33,1},{2,34},{34,2},{3,35},{35,3},{4,36},{36... | collective-permute-start | bytes 24584 | tf_op jit(solution)/shard_map/ppermute | solution.py:261
  104.0 12.1 %collective-permute-start.10 = (bf16[1280,128]{1,0:T(8,128)(2,1)S(1)}, bf16[1280,128]{1,0:T(8,128)(2,1)S(1)}, u32[]{:S(2)}, u32[]{:S(2)}) collective-permute-start(bf16[1280,128]{1,0:T(8,128)(2,1)S(1)} %bitcast.17), channel_id=1, source_target_pairs={{0,160},{32,0},{128,32},{160,128},{1,161},{33,1},{129,33},{161,129... | collective-permute-start | bytes 983048 | tf_op jit(solution)/shard_map/ppermute | solution.py:266
  110.6 14.9 %collective-permute-start.9 = (bf16[1280,128]{1,0:T(8,128)(2,1)S(1)}, bf16[1280,128]{1,0:T(8,128)(2,1)S(1)}, u32[]{:S(2)}, u32[]{:S(2)}) collective-permute-start(bf16[1280,128]{1,0:T(8,128)(2,1)S(1)} %bitcast.18), channel_id=1, source_target_pairs={{0,128},{32,160},{128,0},{160,32},{1,129},{33,161},{129,1},{161,33... | collective-permute-start | bytes 983048 | tf_op jit(solution)/shard_map/ppermute | solution.py:266
  111.4 17.4 %collective-permute-start.8 = (bf16[1280,128]{1,0:T(8,128)(2,1)S(1)}, bf16[1280,128]{1,0:T(8,128)(2,1)S(1)}, u32[]{:S(2)}, u32[]{:S(2)}) collective-permute-start(bf16[1280,128]{1,0:T(8,128)(2,1)S(1)} %bitcast.19), channel_id=1, source_target_pairs={{0,32},{32,128},{128,160},{160,0},{1,33},{33,129},{129,161},{161,1... | collective-permute-start | bytes 983048 | tf_op jit(solution)/shard_map/ppermute | solution.py:266
  111.4 17.9 %collective-permute-start.11 = (bf16[1280,128]{1,0:T(8,128)(2,1)S(1)}, bf16[1280,128]{1,0:T(8,128)(2,1)S(1)}, u32[]{:S(2)}, u32[]{:S(2)}) collective-permute-start(bf16[1280,128]{1,0:T(8,128)(2,1)S(1)} %bitcast.20), channel_id=1, source_target_pairs={{0,64},{64,0},{1,65},{65,1},{2,66},{66,2},{3,67},{67,3},{4,68},{68... | collective-permute-start | bytes 983048 | tf_op jit(solution)/shard_map/ppermute | solution.py:261
  116.2 13.1 %collective-permute-start.14 = (bf16[1280,128]{1,0:T(8,128)(2,1)S(1)}, bf16[1280,128]{1,0:T(8,128)(2,1)S(1)}, u32[]{:S(2)}, u32[]{:S(2)}) collective-permute-start(bf16[1280,128]{1,0:T(8,128)(2,1)S(1)} %collective-permute-done.10.refs_3_), channel_id=1, source_target_pairs={{0,64},{64,0},{1,65},{65,1},{2,66},{66,2},{3,67},{67,3},{4,68},{68... | collective-permute-start | bytes 983048 | tf_op jit(solution)/shard_map/ppermute | solution.py:261
  125.6 3.7 %collective-permute-start.13 = (bf16[1280,128]{1,0:T(8,128)(2,1)S(1)}, bf16[1280,128]{1,0:T(8,128)(2,1)S(1)}, u32[]{:S(2)}, u32[]{:S(2)}) collective-permute-start(bf16[1280,128]{1,0:T(8,128)(2,1)S(1)} %collective-permute-done.9.refs_2_), channel_id=1, source_target_pairs={{0,64},{64,0},{1,65},{65,1},{2,66},{66,2},{3,67},{67,3},{4,68},{68... | collective-permute-start | bytes 983048 | tf_op jit(solution)/shard_map/ppermute | solution.py:261
  128.8 1.8 %collective-permute-start.12 = (bf16[1280,128]{1,0:T(8,128)(2,1)S(1)}, bf16[1280,128]{1,0:T(8,128)(2,1)S(1)}, u32[]{:S(2)}, u32[]{:S(2)}) collective-permute-start(bf16[1280,128]{1,0:T(8,128)(2,1)S(1)} %collective-permute-done.8.refs_1_), channel_id=1, source_target_pairs={{0,64},{64,0},{1,65},{65,1},{2,66},{66,2},{3,67},{67,3},{4,68},{68... | collective-permute-start | bytes 983048 | tf_op jit(solution)/shard_map/ppermute | solution.py:261

commit v4 on v3

--- a/solution.py
+++ b/solution.py
@@ -14,6 +14,7 @@
 LANES = 128
 LEAD = 128
 CHUNK = 1024
+BACK = 2048
 STEP = 32
 PART = 40
 TAPS_AT, OUT_AT, GAINS_AT = 512, 3584, 4608
@@ -180,12 +181,12 @@
                         copy.wait()
 
     def back(i, carry):
-        j = n - 1 - i
-        t0 = pl.multiple_of(j * CHUNK, CHUNK)
-        here = pl.ds(t0, CHUNK)
+        j = rows // BACK - 1 - i
+        t0 = pl.multiple_of(j * BACK, BACK)
+        here = pl.ds(t0, BACK)
 
         def block(g, x, h, gc_ref, half, taps_ref, gain, dist):
-            gcs = [gc_ref[pl.ds(t0 + k * dist, CHUNK), :] for k in range(3)]
+            gcs = [gc_ref[pl.ds(t0 + k * dist, BACK), :] for k in range(3)]
             side = jnp.concatenate(gcs, axis=1)
             taps = jnp.concatenate([taps_ref[k * WIDE : (k + 1) * WIDE, :] for k in range(3)], axis=1)
             gh = cols_dot(side, taps)
@@ -197,10 +198,10 @@
             w = gn * gain
             return g + s * (w - normed * mean(w * normed))
 
-        h2 = h2_ref[pl.ds(t0 + LEAD, CHUNK), :]
+        h2 = h2_ref[pl.ds(t0 + LEAD, BACK), :]
         gx1 = block(gx2_ref[here, :], x1_ref[here, :], h2, gc2_ref, 1, taps2_ref, gain2_ref[...], 2 * STEP)
 
-        @pl.when(i == n - 1)
+        @pl.when(i == rows // BACK - 1)
         def _():
             leave(1, True)
 
@@ -209,12 +210,12 @@
         add(0, OUT_AT, rows_dot(a, low))
         gact = cols_dot(low, out1_ref[...])
         gc1_ref[here, :] = jnp.where(a > 0, gact, 0.0).astype(BF)
-        h1 = h1_ref[pl.ds(t0 + LEAD, CHUNK), :]
+        h1 = h1_ref[pl.ds(t0 + LEAD, BACK), :]
         gx0 = block(gx1, x0_ref[here, :].astype(F32), h1, gc1_ref, 0, taps1_ref, gain1_ref[...], STEP)
         add(0, 0, rows_dot(hot_ref[here, :], gx0.astype(BF)))
         return carry
 
-    lax.fori_loop(0, n, back, 0)
+    lax.fori_loop(0, rows // BACK, back, 0)
 
     leave(0, True)
     leave(1, False)

time: 134 us -> 133 us (level)
  no operation moved by 1% of the time
where the time goes in v4:
time: 133 us; the launch traced here: 132 us
  blocking collectives  38.7 us (29%)
  starting transfers between devices  36.8 us (28%)
  Pallas kernels  26.6 us (20%)
  waiting for transfers between devices  26.3 us (20%)
  other arithmetic  2.35 us (2%)
    pallas_call x1, Pallas kernels, compute(): pl.pallas_call(functools.partial(kernel, peers, loss_scale), out_shape=[j...  24 us
    all_to_all x1, blocking collectives, local(): both = lax.all_to_all(both, ctx, 0, 0, tiled=True)  21.2 us
    ppermute x9, starting transfers between devices, swap(): return lax.ppermute(array, axis, [(i, i ^ mask) for i in range(count)])  19.8 us
    all_to_all x1, blocking collectives, reduce_all(): got = lax.all_to_all(message, rest, 0, 0, tiled=True)  17.5 us
    ppermute x6, waiting for transfers between devices, shift(): lax.ppermute(array, axis, [(i, (i + by) % count) for i in range(count)])  17.2 us
    ppermute x6, starting transfers between devices, shift(): lax.ppermute(array, axis, [(i, (i + by) % count) for i in range(count)])  12.8 us
    all_to_all x1, waiting for transfers between devices, reduce_all(): whole = lax.all_to_all(whole, rest, 0, 0, tiled=True).reshape(-1, LANES)  5.19 us
    all_to_all x1, starting transfers between devices, reduce_all(): whole = lax.all_to_all(whole, rest, 0, 0, tiled=True).reshape(-1, LANES)  4.25 us
  transfers between devices with their start and end apart: 16, of which 9 were waited for; matrix products, arithmetic and copies ran while one was open for 1% of the time, Pallas kernels for 0%

profile of v4, /device:TPU:33, one launch (start us, length us, event | category | flops | bytes accessed | tf_op | source)
XLA Modules:
  0.0 132.3 jit_solution(3219495657595636506)
XLA Ops:
  0.6 0.7 pad_add_fusion
  1.4 21.2 %all_to_all.15.both_ref = s32[64,2,128]{2,1,0:T(2,128)} all-to-all(s32[64,2,128]{2,1,0:T(2,128)S(1)} %bitcast.27), channel_id=1, replica_groups=mesh['x_hi'=2,'core'=2,'x_lo'=2,'y'=4,'z'=8] {'x_lo','y','z'}, dimensions={0} | all-to-all | bytes 131072 | tf_op jit(solution)/shard_map/all_to_all | solution.py:356
  22.6 24.0 %shard_map.186 = (bf16[32,128]{1,0:T(8,128)(2,1)}, f32[1280,128]{1,0:T(8,128)}, f32[1280,128]{1,0:T(8,128)}, f32[1280,128]{1,0:T(8,128)}, f32[1280,128]{1,0:T(8,...) custom-call(s32[64,2,128]{2,1,0:T(2,128)} %all_to_all.15.both_ref, ...), custom_call_target="tpu_custom_call" | custom-call | tf_op jit(solution)/shard_map/pallas_call | solution.py:231
  46.6 0.0 copy-start.2
  46.6 2.0 %collective-permute-start.1 = (f32[1280,128]{1,0:T(8,128)}, f32[1280,128]{1,0:T(8,128)S(1)}, u32[]{:S(2)}, u32[]{:S(2)}) collective-permute-start(f32[1280,128]{1,0:T(8,128)} %get-tuple-element.34), channel_id=1, source_target_pairs={{0,64},{64,0},{1,65},{65,1},{2,66},{66,2},{3,67},{67,3},{4,68},{68... | collective-permute-start | bytes 1966088 | tf_op jit(solution)/shard_map/ppermute | solution.py:262
  48.6 0.1 collective-permute-start.3
  48.7 0.4 collective-permute-start
  49.1 0.1 collective-permute-start.5
  49.2 1.3 %collective-permute-done.1 = f32[1280,128]{1,0:T(8,128)S(1)} collective-permute-done((f32[1280,128]{1,0:T(8,128)}, f32[1280,128]{1,0:T(8,128)S(1)}, u32[]{:S(2)}, u32[]{:S(2)}) %collective-permute-start.1) | collective-permute-done | bytes 655392 | tf_op jit(solution)/shard_map/ppermute | solution.py:262
  50.5 0.0 copy-start.1
  50.5 1.2 add_convert_fusion.3
  51.7 0.7 collective-permute-start.2
  52.4 0.0 collective-permute-done.3
  52.4 0.0 copy-done.2
  52.4 0.0 copy-start
  52.4 0.1 add_convert_fusion.2
  52.5 2.5 %collective-permute-start.4 = (bf16[1280,128]{1,0:T(8,128)(2,1)S(1)}, bf16[1280,128]{1,0:T(8,128)(2,1)S(1)}, u32[]{:S(2)}, u32[]{:S(2)}) collective-permute-start(bf16[1280,128]{1,0:T(8,128)(2,1)S(1)} %add_convert_fusion.2), channel_id=1, source_target_pairs={{0,128},{32,160},{128,0},{160,32},{1,129},{33,161},{129,1},{161,33... | collective-permute-start | bytes 983048 | tf_op jit(solution)/shard_map/ppermute | solution.py:267
  55.0 0.0 collective-permute-done.5
  55.0 0.0 copy-done.1
  55.0 0.1 add_convert_fusion.1
  55.1 0.0 copy-start.3
  55.1 1.8 %collective-permute-start.6 = (bf16[1280,128]{1,0:T(8,128)(2,1)S(1)}, bf16[1280,128]{1,0:T(8,128)(2,1)S(1)}, u32[]{:S(2)}, u32[]{:S(2)}) collective-permute-start(bf16[1280,128]{1,0:T(8,128)(2,1)S(1)} %add_convert_fusion.1), channel_id=1, source_target_pairs={{0,160},{32,0},{128,32},{160,128},{1,161},{33,1},{129,33},{161,129... | collective-permute-start | bytes 983048 | tf_op jit(solution)/shard_map/ppermute | solution.py:267
  56.9 0.0 collective-permute-done
  56.9 5.1 %collective-permute-done.2 = bf16[1280,128]{1,0:T(8,128)(2,1)S(1)} collective-permute-done((bf16[1280,128]{1,0:T(8,128)(2,1)S(1)}, bf16[1280,128]{1,0:T(8,128)(2,1)S(1)}, u32[]{:S(2)}, u32[]{:S(2)}) %collective-permute-start.2) | collective-permute-done | bytes 327712 | tf_op jit(solution)/shard_map/ppermute | solution.py:267
  61.9 7.4 %collective-permute-done.4 = bf16[1280,128]{1,0:T(8,128)(2,1)S(1)} collective-permute-done((bf16[1280,128]{1,0:T(8,128)(2,1)S(1)}, bf16[1280,128]{1,0:T(8,128)(2,1)S(1)}, u32[]{:S(2)}, u32[]{:S(2)}) %collective-permute-start.4) | collective-permute-done | bytes 327712 | tf_op jit(solution)/shard_map/ppermute | solution.py:267
  69.3 0.1 collective-permute-done.6
  69.4 0.0 copy-done
  69.4 0.2 add_convert_fusion
  69.6 0.0 copy-done.3
  69.7 17.5 %all_to_all.16 = bf16[32,48,128]{2,1,0:T(8,128)(2,1)S(1)} all-to-all(bf16[32,48,128]{2,1,0:T(8,128)(2,1)S(1)} %pad_maximum_fusion), channel_id=1, replica_groups=mesh['x_hi'=2,'core'=2,'x_lo'=2,'y'=4,'z'=8] {'y','z'}, dimensions={0} | all-to-all | bytes 786432 | tf_op jit(solution)/shard_map/all_to_all | solution.py:279
  87.2 0.1 slice_reduce_fusion
  87.2 0.8 broadcast_in_dim.32
  88.0 4.2 %all-to-all-start.2 = ((bf16[32,40,128]{2,1,0:T(8,128)(2,1)}), bf16[32,40,128]{2,1,0:T(8,128)(2,1)S(1)}, u32[]{:S(2)}, u32[]{:S(2)}) async-start(bf16[32,40,128]{2,1,0:T(8,128)(2,1)} %broadcast_in_dim.32), calls=%async_computation.2 | async-start | bytes 655360 | tf_op jit(solution)/shard_map/all_to_all | solution.py:283
  92.3 4.4 %collective-permute-start.7 = (bf16[32,128]{1,0:T(8,128)(2,1)S(1)}, bf16[32,128]{1,0:T(8,128)(2,1)S(1)}, u32[]{:S(2)}, u32[]{:S(2)}) collective-permute-start(bf16[32,128]{1,0:T(8,128)(2,1)S(1)} %bitcast.22), channel_id=1, source_target_pairs={{0,32},{32,0},{1,33},{33,1},{2,34},{34,2},{3,35},{35,3},{4,36},{36... | collective-permute-start | bytes 24584 | tf_op jit(solution)/shard_map/ppermute | solution.py:262
  96.6 1.3 %collective-permute-done.7.refs_9_ = bf16[32,128]{1,0:T(8,128)(2,1)S(1)} collective-permute-done((bf16[32,128]{1,0:T(8,128)(2,1)S(1)}, bf16[32,128]{1,0:T(8,128)(2,1)S(1)}, u32[]{:S(2)}, u32[]{:S(2)}) %collective-permute-start.7) | collective-permute-done | bytes 8224 | tf_op jit(solution)/shard_map/ppermute | solution.py:262
  98.0 5.2 %all-to-all-done.2 = bf16[32,40,128]{2,1,0:T(8,128)(2,1)S(1)} async-done(((bf16[32,40,128]{2,1,0:T(8,128)(2,1)}), bf16[32,40,128]{2,1,0:T(8,128)(2,1)S(1)}, u32[]{:S(2)}, u32[]{:S(2)}) %all-to-all-start.2) | async-done | bytes 327712 | tf_op jit(solution)/shard_map/all_to_all | solution.py:283
  103.2 6.6 %collective-permute-start.10 = (bf16[1280,128]{1,0:T(8,128)(2,1)S(1)}, bf16[1280,128]{1,0:T(8,128)(2,1)S(1)}, u32[]{:S(2)}, u32[]{:S(2)}) collective-permute-start(bf16[1280,128]{1,0:T(8,128)(2,1)S(1)} %bitcast.17), channel_id=1, source_target_pairs={{0,160},{32,0},{128,32},{160,128},{1,161},{33,1},{129,33},{161,129... | collective-permute-start | bytes 983048 | tf_op jit(solution)/shard_map/ppermute | solution.py:267
  109.8 1.2 collective-permute-start.9
  111.0 0.0 collective-permute-start.8
  111.0 2.7 %collective-permute-start.11 = (bf16[1280,128]{1,0:T(8,128)(2,1)S(1)}, bf16[1280,128]{1,0:T(8,128)(2,1)S(1)}, u32[]{:S(2)}, u32[]{:S(2)}) collective-permute-start(bf16[1280,128]{1,0:T(8,128)(2,1)S(1)} %bitcast.20), channel_id=1, source_target_pairs={{0,64},{64,0},{1,65},{65,1},{2,66},{66,2},{3,67},{67,3},{4,68},{68... | collective-permute-start | bytes 983048 | tf_op jit(solution)/shard_map/ppermute | solution.py:262
  113.7 1.4 %collective-permute-done.10.refs_3_ = bf16[1280,128]{1,0:T(8,128)(2,1)S(1)} collective-permute-done((bf16[1280,128]{1,0:T(8,128)(2,1)S(1)}, bf16[1280,128]{1,0:T(8,128)(2,1)S(1)}, u32[]{:S(2)}, u32[]{:S(2)}) %collective-permute-start.10) | collective-permute-done | bytes 327712 | tf_op jit(solution)/shard_map/ppermute | solution.py:267
  115.2 9.6 %collective-permute-start.14 = (bf16[1280,128]{1,0:T(8,128)(2,1)S(1)}, bf16[1280,128]{1,0:T(8,128)(2,1)S(1)}, u32[]{:S(2)}, u32[]{:S(2)}) collective-permute-start(bf16[1280,128]{1,0:T(8,128)(2,1)S(1)} %collective-permute-done.10.refs_3_), channel_id=1, source_target_pairs={{0,64},{64,0},{1,65},{65,1},{2,66},{66,2},{3,67},{67,3},{4,68},{68... | collective-permute-start | bytes 983048 | tf_op jit(solution)/shard_map/ppermute | solution.py:262
  124.8 0.0 collective-permute-done.9.refs_2_
  124.8 0.0 collective-permute-start.13
  124.8 3.2 %collective-permute-done.8.refs_1_ = bf16[1280,128]{1,0:T(8,128)(2,1)S(1)} collective-permute-done((bf16[1280,128]{1,0:T(8,128)(2,1)S(1)}, bf16[1280,128]{1,0:T(8,128)(2,1)S(1)}, u32[]{:S(2)}, u32[]{:S(2)}) %collective-permute-start.8) | collective-permute-done | bytes 327712 | tf_op jit(solution)/shard_map/ppermute | solution.py:267
  127.9 0.5 collective-permute-start.12
  128.4 0.0 collective-permute-done.11.refs_4_
  128.4 0.0 collective-permute-done.14.refs_7_
  128.4 0.0 collective-permute-done.13.refs_6_
  128.5 1.2 collective-permute-done.12.refs_5_
  129.7 2.6 %shard_map.187 = (f32[16,128]{1,0:T(8,128)}, f32[256,256]{1,0:T(8,128)}, f32[1,256]{1,0:T(1,128)}, f32[3,256,512]{2,1,0:T(8,128)}, f32[512,256]{1,0:T(8,128)}, /...) custom-call(bf16[1280,128]{1,0:T(8,128)(2,1)S(1)} %bitcast.21, ...), custom_call_target="tpu_custom_call" | custom-call | tf_op jit(solution)/shard_map/pallas_call | solution.py:339
  (6 shorter events, 0.1 us)
Async XLA Ops:
  46.6 5.8 %copy-start.2 = (f32[1280,128]{1,0:T(8,128)S(1)}, f32[1280,128]{1,0:T(8,128)}, u32[]{:S(2)}) copy-start(f32[1280,128]{1,0:T(8,128)} %get-tuple-element.35) | copy-start | bytes 1966084
  46.6 3.9 %collective-permute-start.1 = (f32[1280,128]{1,0:T(8,128)}, f32[1280,128]{1,0:T(8,128)S(1)}, u32[]{:S(2)}, u32[]{:S(2)}) collective-permute-start(f32[1280,128]{1,0:T(8,128)} %get-tuple-element.34), channel_id=1, source_target_pairs={{0,64},{64,0},{1,65},{65,1},{2,66},{66,2},{3,67},{67,3},{4,68},{68... | collective-permute-start | bytes 1966088 | tf_op jit(solution)/shard_map/ppermute | solution.py:262
  48.6 3.8 %collective-permute-start.3 = (f32[1280,128]{1,0:T(8,128)}, f32[1280,128]{1,0:T(8,128)S(1)}, u32[]{:S(2)}, u32[]{:S(2)}) collective-permute-start(f32[1280,128]{1,0:T(8,128)} %get-tuple-element.36), channel_id=1, source_target_pairs={{0,64},{64,0},{1,65},{65,1},{2,66},{66,2},{3,67},{67,3},{4,68},{68... | collective-permute-start | bytes 1966088 | tf_op jit(solution)/shard_map/ppermute | solution.py:262
  48.7 8.2 %collective-permute-start = (f32[1280,128]{1,0:T(8,128)}, f32[1280,128]{1,0:T(8,128)S(1)}, u32[]{:S(2)}, u32[]{:S(2)}) collective-permute-start(f32[1280,128]{1,0:T(8,128)} %get-tuple-element.32), channel_id=1, source_target_pairs={{0,64},{64,0},{1,65},{65,1},{2,66},{66,2},{3,67},{67,3},{4,68},{68... | collective-permute-start | bytes 1966088 | tf_op jit(solution)/shard_map/ppermute | solution.py:262
  49.1 5.9 %collective-permute-start.5 = (f32[1280,128]{1,0:T(8,128)}, f32[1280,128]{1,0:T(8,128)S(1)}, u32[]{:S(2)}, u32[]{:S(2)}) collective-permute-start(f32[1280,128]{1,0:T(8,128)} %get-tuple-element.38), channel_id=1, source_target_pairs={{0,64},{64,0},{1,65},{65,1},{2,66},{66,2},{3,67},{67,3},{4,68},{68... | collective-permute-start | bytes 1966088 | tf_op jit(solution)/shard_map/ppermute | solution.py:262
  50.5 4.5 %copy-start.1 = (f32[1280,128]{1,0:T(8,128)S(1)}, f32[1280,128]{1,0:T(8,128)}, u32[]{:S(2)}) copy-start(f32[1280,128]{1,0:T(8,128)} %get-tuple-element.37) | copy-start | bytes 1966084
  51.7 10.2 %collective-permute-start.2 = (bf16[1280,128]{1,0:T(8,128)(2,1)S(1)}, bf16[1280,128]{1,0:T(8,128)(2,1)S(1)}, u32[]{:S(2)}, u32[]{:S(2)}) collective-permute-start(bf16[1280,128]{1,0:T(8,128)(2,1)S(1)} %add_convert_fusion.3), channel_id=1, source_target_pairs={{0,32},{32,128},{128,160},{160,0},{1,33},{33,129},{129,161},{161,1... | collective-permute-start | bytes 983048 | tf_op jit(solution)/shard_map/ppermute | solution.py:267
  52.4 17.0 %copy-start = (f32[1280,128]{1,0:T(8,128)S(1)}, f32[1280,128]{1,0:T(8,128)}, u32[]{:S(2)}) copy-start(f32[1280,128]{1,0:T(8,128)} %get-tuple-element.31) | copy-start | bytes 1966084
  52.5 16.9 %collective-permute-start.4 = (bf16[1280,128]{1,0:T(8,128)(2,1)S(1)}, bf16[1280,128]{1,0:T(8,128)(2,1)S(1)}, u32[]{:S(2)}, u32[]{:S(2)}) collective-permute-start(bf16[1280,128]{1,0:T(8,128)(2,1)S(1)} %add_convert_fusion.2), channel_id=1, source_target_pairs={{0,128},{32,160},{128,0},{160,32},{1,129},{33,161},{129,1},{161,33... | collective-permute-start | bytes 983048 | tf_op jit(solution)/shard_map/ppermute | solution.py:267
  55.1 14.5 %copy-start.3 = (bf16[32,128]{1,0:T(8,128)(2,1)S(1)}, bf16[32,128]{1,0:T(8,128)(2,1)}, u32[]{:S(2)}) copy-start(bf16[32,128]{1,0:T(8,128)(2,1)} %get-tuple-element.39) | copy-start | bytes 24580
  55.1 14.3 %collective-permute-start.6 = (bf16[1280,128]{1,0:T(8,128)(2,1)S(1)}, bf16[1280,128]{1,0:T(8,128)(2,1)S(1)}, u32[]{:S(2)}, u32[]{:S(2)}) collective-permute-start(bf16[1280,128]{1,0:T(8,128)(2,1)S(1)} %add_convert_fusion.1), channel_id=1, source_target_pairs={{0,160},{32,0},{128,32},{160,128},{1,161},{33,1},{129,33},{161,129... | collective-permute-start | bytes 983048 | tf_op jit(solution)/shard_map/ppermute | solution.py:267
  88.0 15.2 %all-to-all-start.2 = ((bf16[32,40,128]{2,1,0:T(8,128)(2,1)}), bf16[32,40,128]{2,1,0:T(8,128)(2,1)S(1)}, u32[]{:S(2)}, u32[]{:S(2)}) async-start(bf16[32,40,128]{2,1,0:T(8,128)(2,1)} %broadcast_in_dim.32), calls=%async_computation.2 | async-start | bytes 655360 | tf_op jit(solution)/shard_map/all_to_all | solution.py:283
  92.3 5.7 %collective-permute-start.7 = (bf16[32,128]{1,0:T(8,128)(2,1)S(1)}, bf16[32,128]{1,0:T(8,128)(2,1)S(1)}, u32[]{:S(2)}, u32[]{:S(2)}) collective-permute-start(bf16[32,128]{1,0:T(8,128)(2,1)S(1)} %bitcast.22), channel_id=1, source_target_pairs={{0,32},{32,0},{1,33},{33,1},{2,34},{34,2},{3,35},{35,3},{4,36},{36... | collective-permute-start | bytes 24584 | tf_op jit(solution)/shard_map/ppermute | solution.py:262
  103.2 12.0 %collective-permute-start.10 = (bf16[1280,128]{1,0:T(8,128)(2,1)S(1)}, bf16[1280,128]{1,0:T(8,128)(2,1)S(1)}, u32[]{:S(2)}, u32[]{:S(2)}) collective-permute-start(bf16[1280,128]{1,0:T(8,128)(2,1)S(1)} %bitcast.17), channel_id=1, source_target_pairs={{0,160},{32,0},{128,32},{160,128},{1,161},{33,1},{129,33},{161,129... | collective-permute-start | bytes 983048 | tf_op jit(solution)/shard_map/ppermute | solution.py:267
  109.8 15.0 %collective-permute-start.9 = (bf16[1280,128]{1,0:T(8,128)(2,1)S(1)}, bf16[1280,128]{1,0:T(8,128)(2,1)S(1)}, u32[]{:S(2)}, u32[]{:S(2)}) collective-permute-start(bf16[1280,128]{1,0:T(8,128)(2,1)S(1)} %bitcast.18), channel_id=1, source_target_pairs={{0,128},{32,160},{128,0},{160,32},{1,129},{33,161},{129,1},{161,33... | collective-permute-start | bytes 983048 | tf_op jit(solution)/shard_map/ppermute | solution.py:267
  111.0 16.9 %collective-permute-start.8 = (bf16[1280,128]{1,0:T(8,128)(2,1)S(1)}, bf16[1280,128]{1,0:T(8,128)(2,1)S(1)}, u32[]{:S(2)}, u32[]{:S(2)}) collective-permute-start(bf16[1280,128]{1,0:T(8,128)(2,1)S(1)} %bitcast.19), channel_id=1, source_target_pairs={{0,32},{32,128},{128,160},{160,0},{1,33},{33,129},{129,161},{161,1... | collective-permute-start | bytes 983048 | tf_op jit(solution)/shard_map/ppermute | solution.py:267
  111.0 17.4 %collective-permute-start.11 = (bf16[1280,128]{1,0:T(8,128)(2,1)S(1)}, bf16[1280,128]{1,0:T(8,128)(2,1)S(1)}, u32[]{:S(2)}, u32[]{:S(2)}) collective-permute-start(bf16[1280,128]{1,0:T(8,128)(2,1)S(1)} %bitcast.20), channel_id=1, source_target_pairs={{0,64},{64,0},{1,65},{65,1},{2,66},{66,2},{3,67},{67,3},{4,68},{68... | collective-permute-start | bytes 983048 | tf_op jit(solution)/shard_map/ppermute | solution.py:262
  115.2 13.3 %collective-permute-start.14 = (bf16[1280,128]{1,0:T(8,128)(2,1)S(1)}, bf16[1280,128]{1,0:T(8,128)(2,1)S(1)}, u32[]{:S(2)}, u32[]{:S(2)}) collective-permute-start(bf16[1280,128]{1,0:T(8,128)(2,1)S(1)} %collective-permute-done.10.refs_3_), channel_id=1, source_target_pairs={{0,64},{64,0},{1,65},{65,1},{2,66},{66,2},{3,67},{67,3},{4,68},{68... | collective-permute-start | bytes 983048 | tf_op jit(solution)/shard_map/ppermute | solution.py:262
  124.8 3.7 %collective-permute-start.13 = (bf16[1280,128]{1,0:T(8,128)(2,1)S(1)}, bf16[1280,128]{1,0:T(8,128)(2,1)S(1)}, u32[]{:S(2)}, u32[]{:S(2)}) collective-permute-start(bf16[1280,128]{1,0:T(8,128)(2,1)S(1)} %collective-permute-done.9.refs_2_), channel_id=1, source_target_pairs={{0,64},{64,0},{1,65},{65,1},{2,66},{66,2},{3,67},{67,3},{4,68},{68... | collective-permute-start | bytes 983048 | tf_op jit(solution)/shard_map/ppermute | solution.py:262
  127.9 1.8 %collective-permute-start.12 = (bf16[1280,128]{1,0:T(8,128)(2,1)S(1)}, bf16[1280,128]{1,0:T(8,128)(2,1)S(1)}, u32[]{:S(2)}, u32[]{:S(2)}) collective-permute-start(bf16[1280,128]{1,0:T(8,128)(2,1)S(1)} %collective-permute-done.8.refs_1_), channel_id=1, source_target_pairs={{0,64},{64,0},{1,65},{65,1},{2,66},{66,2},{3,67},{67,3},{4,68},{68... | collective-permute-start | bytes 983048 | tf_op jit(solution)/shard_map/ppermute | solution.py:262
